TPU v7x, 32 devices: a whole 2x2x4 slice. The times are simulated.
32 devices in a mesh: section: 2 (over core), dp: 4 (over y, x), seq: 4 (over z).
Axes of the slice: x: 2, y: 2, z: 4, core: 2. Of those that a mesh axis runs over, the one named last changes fastest.
Arguments:
- inputs: bfloat16 [2, 4, 2048, 512], P(None, 'dp', 'seq'), may hold values from -6 to 6
- cotangent: bfloat16 [2, 4, 2048, 512], P(None, 'dp', 'seq'), may hold values from -6 to 6
- doc_lengths: int32 [2, 4, 4], P(None, 'dp'), may hold values from 1 to 2045, as said below
- feature_proj: float32 [2, 8, 64, 256], P('section'), may hold values from -6 to 6
- w_query: float32 [2, 512, 512], P('section', ('dp', 'seq')), may hold values from -0.25 to 0.25
- w_key: float32 [2, 512, 512], P('section', ('dp', 'seq')), may hold values from -0.25 to 0.25
- w_value: float32 [2, 512, 512], P('section', ('dp', 'seq')), may hold values from -0.25 to 0.25
- w_out: float32 [2, 512, 512], P('section', ('dp', 'seq')), may hold values from -1.5 to 1.5
- w_up: float32 [2, 512, 2048], P('section', ('dp', 'seq')), may hold values from -0.25 to 0.25
- w_down: float32 [2, 2048, 512], P('section', ('dp', 'seq')), may hold values from -0.125 to 0.125
- gain_attn: float32 [2, 512], P('section', ('dp', 'seq')), may hold values from 0.1 to 1.9
- gain_ffn: float32 [2, 512], P('section', ('dp', 'seq')), may hold values from 0.1 to 1.9
Outputs:
- activations: bfloat16 [2, 2, 4, 2048, 512], P('section', None, 'dp', 'seq')
- input_grad: bfloat16 [2, 2, 4, 2048, 512], P('section', None, 'dp', 'seq')
- grad_query: float32 [2, 512, 512], P('section', ('dp', 'seq'))
- grad_key: float32 [2, 512, 512], P('section', ('dp', 'seq'))
- grad_value: float32 [2, 512, 512], P('section', ('dp', 'seq'))
- grad_out: float32 [2, 512, 512], P('section', ('dp', 'seq'))
- grad_up: float32 [2, 512, 2048], P('section', ('dp', 'seq'))
- grad_down: float32 [2, 2048, 512], P('section', ('dp', 'seq'))
- grad_gain_attn: float32 [2, 512], P('section', ('dp', 'seq'))
- grad_gain_ffn: float32 [2, 512], P('section', ('dp', 'seq'))
Inputs may be any that keep to these rules, and one draw needn't show every extreme that they name: `doc_lengths`: each row of 4 lengths sums to 2048; its second document covers the positions 256 to 1791.
All inputs are finite; a program needn't handle non-finite values.
Results may differ from a plain program's by a relative error of at most 0.023.
The roundings to bfloat16 on the way count: a program that leaves them out, or rounds other values in their place, can miss the bound.
Values may be sent and summed in bfloat16 or wider, within the bound.
A program may use at most 256 MiB of HBM per device.

v0:
```python
import jax
import jax.numpy as jnp
from jax import lax
from jax.sharding import PartitionSpec as P

HIGH_PRECISION = lax.Precision.HIGHEST


def prefix(shard, axis, join, neutral):
    place = lax.axis_index(axis)
    gathered = jax.tree.map(
        lambda a, kind: lax.all_gather(a.astype(kind), axis),
        shard,
        (jnp.bfloat16, jnp.bfloat16, jnp.bfloat16),
    )
    state = jax.tree.map(lambda a, e: jnp.zeros_like(a) + jnp.asarray(e, a.dtype), shard, neutral)

    def prefix_one(lap, state):
        return join(
            state,
            jax.tree.map(
                lambda a, own: lax.dynamic_index_in_dim(a, lap, 0, False).astype(own.dtype),
                gathered,
                shard,
            ),
        )

    return lax.fori_loop(0, place, prefix_one, state)


def entering(shard, axis, join, neutral):
    count = lax.axis_size(axis)
    place = lax.axis_index(axis)
    ahead = count - 1 - place
    gathered = jax.tree.map(
        lambda a, kind: lax.all_gather(a.astype(kind), axis),
        shard,
        jax.tree.map(lambda a: jnp.bfloat16 if a.dtype == jnp.float32 else a.dtype, shard),
    )
    state = jax.tree.map(lambda a, e: jnp.zeros_like(a) + jnp.asarray(e, a.dtype), shard, neutral)

    def entering_one(lap, state):
        source = count - 1 - lap
        return join(
            state,
            jax.tree.map(
                lambda a, own: lax.dynamic_index_in_dim(a, source, 0, False).astype(own.dtype),
                gathered,
                shard,
            ),
        )

    return lax.fori_loop(0, ahead, entering_one, state)


def as_sent(shard):

    def short(part):
        return part.astype(jnp.bfloat16) if part.dtype == jnp.float32 else part

    return jax.tree.map(short, shard)


def passed_along(block, axis, distance):
    devices = range(lax.axis_size(axis))
    route = [(i - distance, i) for i in devices if i - distance in devices]
    return lax.ppermute(block, axis, route)


def matmul(left, right):
    return jnp.dot(left, right, preferred_element_type=jnp.float32)


def norm_rows(values):
    centre = values - jnp.mean(values, axis=-1, keepdims=True)
    return centre * lax.rsqrt(jnp.mean(centre * centre, axis=-1, keepdims=True) + 1e-05)


def lift(values, projection):
    heads, depth, feats = projection.shape
    scaled = values.reshape(values.shape[0], heads, depth) * depth ** (-0.25)
    raised = jnp.einsum("nhd,hdm->nhm", scaled, projection, precision=HIGH_PRECISION)
    return jnp.exp(raised - 0.5 * jnp.sum(scaled * scaled, axis=-1, keepdims=True)) * feats ** (
        -0.5
    )


def doc_masks(lengths, first_row, row_count):
    doc_ends = jnp.cumsum(lengths, dtype=jnp.int32)
    starts = doc_ends - lengths
    positions = first_row + jnp.arange(row_count, dtype=jnp.int32)
    begun_at = starts[None, :] <= positions[:, None]
    doc_ids = jnp.sum(begun_at.astype(jnp.int32), axis=1)
    order_idx = jnp.arange(row_count, dtype=jnp.int32)
    same_doc = (
        (doc_ids[:, None] == doc_ids[None, :]) & (order_idx[None, :] <= order_idx[:, None])
    ).astype(jnp.float32)
    inside = (starts >= first_row) & (starts < first_row + row_count)
    mask_per_head = (jnp.sum((begun_at & inside[None, :]).astype(jnp.int32), axis=1) == 0).astype(
        jnp.float32
    )
    tail_mask = (jnp.sum((~begun_at & inside[None, :]).astype(jnp.int32), axis=1) == 0).astype(
        jnp.float32
    )
    kept_flag = (jnp.sum(inside.astype(jnp.int32)) == 0).astype(jnp.float32)
    return (same_doc, mask_per_head, tail_mask, kept_flag)


def attend(query_features, feats_k, value_heads, incoming_state, norm_in, same_doc, mask_per_head):
    scores = (
        jnp.einsum("thm,shm->hts", query_features, feats_k, precision=HIGH_PRECISION)
        * same_doc[None]
    )
    attention_numerator = jnp.einsum("hts,shd->thd", scores, value_heads, precision=HIGH_PRECISION)
    attention_numerator = attention_numerator + mask_per_head[:, None, None] * jnp.einsum(
        "kec,ecz->kez", query_features, incoming_state, precision=HIGH_PRECISION
    )
    denominator = jnp.sum(scores, axis=2).T + mask_per_head[:, None] * jnp.einsum(
        "thm,hm->th", query_features, norm_in, precision=HIGH_PRECISION
    )
    return (attention_numerator / denominator[:, :, None]).reshape(query_features.shape[0], -1)


def tail_sums(feats_k, value_heads, tail_mask):
    weighted_values = feats_k * tail_mask[:, None, None]
    return (
        jnp.einsum("zlu,zlv->luv", weighted_values, value_heads, precision=HIGH_PRECISION),
        jnp.sum(weighted_values, axis=0),
    )


def combine_carry(earlier, later_part):
    return (
        earlier[0] * later_part[0],
        later_part[1] + later_part[0] * earlier[1],
        later_part[2] + later_part[0] * earlier[2],
    )


def run_forward(layer_in, weights, projection, lengths, first_row):
    w_query, w_key, w_value, w_out, w_up, w_down, gain_attn, gain_ffn = weights
    row_count = layer_in.shape[0]
    same_doc, mask_per_head, tail_mask, kept_flag = doc_masks(lengths, first_row, row_count)
    h_attn = (norm_rows(layer_in) * gain_attn.astype(jnp.float32)).astype(jnp.bfloat16)
    query_features = lift(matmul(h_attn, w_query), projection)
    feats_k = lift(matmul(h_attn, w_key), projection)
    value_heads = matmul(h_attn, w_value).reshape(row_count, projection.shape[0], -1)
    state_tail, norm_tail = tail_sums(feats_k, value_heads, tail_mask)
    identity = (jnp.ones((), jnp.float32), jnp.zeros_like(state_tail), jnp.zeros_like(norm_tail))
    _, incoming_state, norm_in = prefix(
        (kept_flag, state_tail, norm_tail), "seq", combine_carry, identity
    )
    mixed_heads = attend(
        query_features, feats_k, value_heads, incoming_state, norm_in, same_doc, mask_per_head
    ).astype(jnp.bfloat16)
    branch = layer_in + matmul(mixed_heads, w_out)
    h_ffn = (norm_rows(branch) * gain_ffn.astype(jnp.float32)).astype(jnp.bfloat16)
    hidden = jax.nn.gelu(matmul(h_ffn, w_up)).astype(jnp.bfloat16)
    return (branch + matmul(hidden, w_down), incoming_state, norm_in)


def run_backward(
    layer_in, incoming_state, norm_in, grad_out, weights, projection, lengths, first_row
):
    w_query, w_key, w_value, w_out, w_up, w_down, gain_attn, gain_ffn = weights
    row_count = layer_in.shape[0]
    same_doc, mask_per_head, tail_mask, kept_flag = doc_masks(lengths, first_row, row_count)
    gain_a = gain_attn.astype(jnp.float32)
    gain_f = gain_ffn.astype(jnp.float32)
    normed_a, norm_a_back = jax.vjp(norm_rows, layer_in)
    h_attn = (normed_a * gain_a).astype(jnp.bfloat16)
    query_features, lift_q_back = jax.vjp(lambda z: lift(z, projection), matmul(h_attn, w_query))
    feats_k, lift_k_back = jax.vjp(lambda z: lift(z, projection), matmul(h_attn, w_key))
    value_heads = matmul(h_attn, w_value).reshape(row_count, projection.shape[0], -1)
    attended, attend_back = jax.vjp(
        lambda a, b, c, d, e: attend(a, b, c, d, e, same_doc, mask_per_head),
        query_features,
        feats_k,
        value_heads,
        incoming_state,
        norm_in,
    )
    mixed_heads = attended.astype(jnp.bfloat16)
    branch = layer_in + matmul(mixed_heads, w_out)
    normed_f, norm_f_back = jax.vjp(norm_rows, branch)
    h_ffn = (normed_f * gain_f).astype(jnp.bfloat16)
    activated, gelu_back = jax.vjp(jax.nn.gelu, matmul(h_ffn, w_up))
    hidden = activated.astype(jnp.bfloat16)
    grad_low = grad_out.astype(jnp.bfloat16)
    grad_wdown = matmul(hidden.T, grad_low)
    grad_pre = gelu_back(matmul(grad_low, w_down.T))[0].astype(jnp.bfloat16)
    grad_wup = matmul(h_ffn.T, grad_pre)
    grad_hffn = matmul(grad_pre, w_up.T)
    grad_gain_f = jnp.sum(grad_hffn * normed_f, axis=0)
    ffn_terms = (grad_wup, grad_wdown, grad_gain_f)
    grad_branch = grad_out + norm_f_back(grad_hffn * gain_f)[0]
    grad_blow = grad_branch.astype(jnp.bfloat16)
    grad_wout = matmul(mixed_heads.T, grad_blow)
    grad_fq, grad_fk, grad_vals, grad_state, grad_norm = attend_back(matmul(grad_blow, w_out.T))
    identity = (jnp.ones((), jnp.float32), jnp.zeros_like(grad_state), jnp.zeros_like(grad_norm))
    _, carry_state, carry_norm = entering(
        (kept_flag, grad_state, grad_norm), "seq", combine_carry, identity
    )
    _, tail_back = jax.vjp(lambda a, b: tail_sums(a, b, tail_mask), feats_k, value_heads)
    more_k, more_v = tail_back((carry_state, carry_norm))
    grad_q = lift_q_back(grad_fq)[0].astype(jnp.bfloat16)
    grad_k = lift_k_back(grad_fk + more_k)[0].astype(jnp.bfloat16)
    grad_v = (grad_vals + more_v).reshape(row_count, -1).astype(jnp.bfloat16)
    grad_hattn = matmul(grad_q, w_query.T) + matmul(grad_k, w_key.T) + matmul(grad_v, w_value.T)
    grad_gain_a = jnp.sum(grad_hattn * normed_a, axis=0)
    grad_in = grad_branch + norm_a_back(grad_hattn * gain_a)[0]
    attn_grads = (
        matmul(h_attn.T, grad_q),
        matmul(h_attn.T, grad_k),
        matmul(h_attn.T, grad_v),
        grad_wout,
        grad_gain_a,
    )
    return (grad_in, attn_grads, ffn_terms)


def local(
    inputs,
    cotangent,
    doc_lengths,
    feature_proj,
    w_query,
    w_key,
    w_value,
    w_out,
    w_up,
    w_down,
    gain_attn,
    gain_ffn,
):
    section_idx = lax.axis_index("section")
    seq_idx = lax.axis_index("seq")
    micro_count, _, row_count, feat_width = inputs.shape
    first_row = seq_idx * row_count
    projection = feature_proj[0]
    lengths_all = doc_lengths[:, 0, :]
    masters = (
        w_query[0],
        w_key[0],
        w_value[0],
        w_out[0],
        w_up[0],
        w_down[0],
        gain_attn[0],
        gain_ffn[0],
    )
    lowered = tuple((master.astype(jnp.bfloat16) for master in masters))
    gathered = jax.tree.map(
        lambda part, own: part.astype(own.dtype),
        lax.all_gather(as_sent(lowered), ("dp", "seq"), axis=0, tiled=True),
        lowered,
    )
    batch_range = jnp.arange(micro_count, dtype=jnp.int32)
    received = jnp.zeros((row_count, feat_width), jnp.bfloat16)
    outputs = jnp.zeros((micro_count, row_count, feat_width), jnp.float32)
    kept_inputs, kept_states, kept_norms = ([], [], [])
    for step_no in range(micro_count + 1):
        batch_no = step_no - section_idx
        is_valid = ((batch_no >= 0) & (batch_no < micro_count)).astype(jnp.float32)
        batch_idx = jnp.clip(batch_no, 0, micro_count - 1)
        own_input = inputs[min(step_no, micro_count - 1), 0].astype(jnp.float32)
        layer_in = jnp.where(section_idx == 0, own_input, received.astype(jnp.float32))
        lengths = lax.dynamic_index_in_dim(lengths_all, batch_idx, 0, keepdims=False)
        layer_out, incoming_state, norm_in = run_forward(
            layer_in, gathered, projection, lengths, first_row
        )
        sent_out = layer_out.astype(jnp.bfloat16)
        chosen = (batch_range == batch_idx).astype(jnp.float32) * is_valid
        outputs = outputs + chosen[:, None, None] * sent_out.astype(jnp.float32)[None]
        kept_inputs.append(layer_in)
        kept_states.append(incoming_state)
        kept_norms.append(norm_in)
        if step_no < micro_count:
            received = passed_along(sent_out, "section", 1)
    weights_back = jax.tree.map(
        lambda part, own: part.astype(own.dtype),
        lax.all_gather(as_sent(lowered), ("dp", "seq"), axis=0, tiled=True),
        lowered,
    )
    stacked_inputs = jnp.stack(kept_inputs)
    stacked_states = jnp.stack(kept_states)
    stacked_norms = jnp.stack(kept_norms)
    grad_recv = jnp.zeros((row_count, feat_width), jnp.bfloat16)
    grad_inputs = jnp.zeros((micro_count, row_count, feat_width), jnp.float32)
    totals = tuple((jnp.zeros(part.shape, jnp.float32) for part in weights_back))
    for step_no in range(micro_count + 1):
        batch_no = step_no - 1 + section_idx
        is_valid = ((batch_no >= 0) & (batch_no < micro_count)).astype(jnp.float32)
        batch_idx = jnp.clip(batch_no, 0, micro_count - 1)
        slot_idx = jnp.clip(step_no - 1 + 2 * section_idx, 0, micro_count)
        layer_in = lax.dynamic_index_in_dim(stacked_inputs, slot_idx, 0, keepdims=False)
        incoming_state = lax.dynamic_index_in_dim(stacked_states, slot_idx, 0, keepdims=False)
        norm_in = lax.dynamic_index_in_dim(stacked_norms, slot_idx, 0, keepdims=False)
        own_grad = cotangent[min(step_no, micro_count - 1), 0].astype(jnp.float32)
        grad_out = jnp.where(section_idx == 1, own_grad, grad_recv.astype(jnp.float32))
        lengths = lax.dynamic_index_in_dim(lengths_all, batch_idx, 0, keepdims=False)
        grad_in, attn_grads, ffn_terms = run_backward(
            layer_in,
            incoming_state,
            norm_in,
            grad_out,
            weights_back,
            projection,
            lengths,
            first_row,
        )
        grads = (
            attn_grads[0],
            attn_grads[1],
            attn_grads[2],
            attn_grads[3],
            ffn_terms[0],
            ffn_terms[1],
            attn_grads[4],
            ffn_terms[2],
        )
        totals = tuple(
            (total_part + is_valid * grad_part for total_part, grad_part in zip(totals, grads))
        )
        sent_back = grad_in.astype(jnp.bfloat16)
        chosen = (batch_range == batch_idx).astype(jnp.float32) * is_valid
        grad_inputs = grad_inputs + chosen[:, None, None] * sent_back.astype(jnp.float32)[None]
        if step_no < micro_count:
            grad_recv = passed_along(sent_back, "section", -1)
    shares = lax.psum_scatter(totals, ("dp", "seq"), scatter_dimension=0, tiled=True)
    activations = outputs.astype(jnp.bfloat16)[None, :, None]
    input_grad = grad_inputs.astype(jnp.bfloat16)[None, :, None]
    return (activations, input_grad) + tuple((share_part[None] for share_part in shares))


def solution(mesh):
    in_specs = (
        P(None, "dp", "seq", None),
        P(None, "dp", "seq", None),
        P(None, "dp", None),
        P("section", None, None, None),
        P("section", ("dp", "seq"), None),
        P("section", ("dp", "seq"), None),
        P("section", ("dp", "seq"), None),
        P("section", ("dp", "seq"), None),
        P("section", ("dp", "seq"), None),
        P("section", ("dp", "seq"), None),
        P("section", ("dp", "seq")),
        P("section", ("dp", "seq")),
    )
    out_specs = (
        P("section", None, "dp", "seq", None),
        P("section", None, "dp", "seq", None),
        P("section", ("dp", "seq"), None),
        P("section", ("dp", "seq"), None),
        P("section", ("dp", "seq"), None),
        P("section", ("dp", "seq"), None),
        P("section", ("dp", "seq"), None),
        P("section", ("dp", "seq"), None),
        P("section", ("dp", "seq")),
        P("section", ("dp", "seq")),
    )
    return jax.shard_map(local, mesh=mesh, in_specs=in_specs, out_specs=out_specs, check_vma=False)
```

profile of v0, /device:TPU:27, one launch (start us, length us, event | category | flops | bytes accessed | tf_op | source)
XLA Modules:
  0.0 1484.2 jit_solution(8470237224165029612)
XLA Ops:
  17.0 29.5 %all-reduce.11 = (bf16[512]{0:T(512)(128)(2,1)S(1)}, bf16[512]{0:T(512)(128)(2,1)S(1)}) all-reduce(bf16[512]{0:T(512)(128)(2,1)S(1)} %dynamic-update-slice, bf16[512]{0:T(512)(128)(2,1)S(1)} %dynamic-update-slice.2), channel_id=2, replica_groups=mesh['section'=2,'dp'=4,'seq'=4] {'dp','seq'}, use_global_device_ids=true, to_apply=%add | all-reduce | flops 1024 | bytes 4096
  46.6 34.7 %all-gather.2 = bf16[1,512,512]{2,1,0:T(8,128)(2,1)S(1)} all-gather(bf16[1,32,512]{2,1,0:T(8,128)(2,1)S(1)} %convert_element_type.893), channel_id=4, replica_groups=mesh['section'=2,'dp'=4,'seq'=4] {'dp','seq'}, dimensions={1}, use_global_device_ids=true | all-gather | bytes 557056 | tf_op jit(solution)/shard_map/all_gather | solution.py:255
  81.6 34.8 %all-gather.3 = bf16[1,512,512]{2,1,0:T(8,128)(2,1)S(1)} all-gather(bf16[1,32,512]{2,1,0:T(8,128)(2,1)S(1)} %convert_element_type.895), channel_id=5, replica_groups=mesh['section'=2,'dp'=4,'seq'=4] {'dp','seq'}, dimensions={1}, use_global_device_ids=true | all-gather | bytes 557056 | tf_op jit(solution)/shard_map/all_gather | solution.py:255
  119.6 34.2 %all-gather.1 = bf16[1,512,512]{2,1,0:T(8,128)(2,1)S(1)} all-gather(bf16[1,32,512]{2,1,0:T(8,128)(2,1)S(1)} %convert_element_type.891), channel_id=3, replica_groups=mesh['section'=2,'dp'=4,'seq'=4] {'dp','seq'}, dimensions={1}, use_global_device_ids=true | all-gather | bytes 557056 | tf_op jit(solution)/shard_map/all_gather | solution.py:255
  169.5 10.8 all-gather.5
  191.8 38.5 %all-gather.6 = bf16[1,512,512]{2,1,0:T(8,128)(2,1)S(1)} all-gather(bf16[1,32,512]{2,1,0:T(8,128)(2,1)S(1)} %convert_element_type.910), channel_id=8, replica_groups=mesh['section'=2,'dp'=4,'seq'=4] {'dp','seq'}, dimensions={1}, use_global_device_ids=true | all-gather | bytes 557056 | tf_op jit(solution)/shard_map/all_gather | solution.py:255
  238.2 12.9 multiply_reduce_fusion.2
  290.6 62.8 %all-gather.33.cloned.1.call-done = bf16[1,2048,512]{2,1,0:T(8,128)(2,1)} async-done(((bf16[1,128,512]{2,1,0:T(8,128)(2,1)}), bf16[1,2048,512]{2,1,0:T(8,128)(2,1)}) %all-gather.33.cloned.1.call-update) | async-done | bytes 2097168 | tf_op jit(solution)/shard_map/all_gather | solution.py:255
  382.4 10.4 all-gather.11
  400.0 10.3 multiply_reduce_fusion.1
  481.2 10.8 all-gather.13
  504.9 10.5 multiply_reduce_fusion.5
  516.5 14.6 while.92
  567.7 10.1 fusion.510
  578.3 17.4 %fusion.7 = f32[8,512,256]{2,1,0:T(8,128)S(1)} fusion(f32[8,512,512]{1,2,0:T(8,128)} %fusion.510, f32[8,512]{1,0:T(8,128)S(1)} %negate_bitcast_fusion.2, f32[512,512]{0,1:T(8,128)S(1)} %copy-done.47, f32[8,512,256]{2,1,0:T(8,128)} %copy-done.19, f32[512,8]{0,1:T(8,128)S(1)} %copy-done.216), kind=kOutput, calls=%fused_computation.31 | convolution fusion | flops 6448742400 | bytes 17858560 | tf_op jit(solution)/shard_map/transpose(jvp(thm,shm->hts))/dot_general | solution.py:111
  605.5 10.5 all-gather.15
  640.3 11.5 fusion.457
  651.8 14.2 fusion.92
  686.7 14.4 collective-permute-start.2
  797.3 10.2 fusion.505
  810.5 15.6 %all-gather.17 = bf16[32,256]{1,0:T(8,128)(2,1)S(1)} all-gather(bf16[8,256]{1,0:T(8,128)(2,1)S(1)} %bitcast.1358), channel_id=19, replica_groups=mesh['section'=2,'dp'=4,'seq'=4] {'seq'}, dimensions={0}, use_global_device_ids=true | all-gather | bytes 20480 | tf_op jit(solution)/shard_map/all_gather | solution.py:36
  826.2 17.5 %fusion.9 = f32[8,512,256]{2,1,0:T(8,128)S(1)} fusion(f32[8,512,512]{1,2,0:T(8,128)} %fusion.505, f32[8,512]{1,0:T(8,128)S(1)} %negate_bitcast_fusion.1, f32[512,512]{0,1:T(8,128)S(1)} %copy-done.43, f32[8,512,256]{2,1,0:T(8,128)} %copy-done.21, f32[512,8]{0,1:T(8,128)S(1)} %get-tuple-element.867), kind=kOutput, calls=%fused_computation.33 | convolution fusion | flops 6448742400 | bytes 17858560 | tf_op jit(solution)/shard_map/transpose(jvp(thm,shm->hts))/dot_general | solution.py:111
  875.5 11.5 fusion.454
  887.1 14.2 fusion.83
  948.2 16.0 %fusion.11 = f32[8,512,256]{2,1,0:T(8,128)} fusion(f32[8,512,512]{1,2,0:T(8,128)S(1)} %fusion.500, f32[8,512]{1,0:T(8,128)S(1)} %negate_bitcast_fusion, f32[512,512]{0,1:T(8,128)S(1)} %copy-done.41, f32[8,512,256]{2,1,0:T(8,128)S(1)} %copy-done.17, f32[512,8]{0,1:T(8,128)S(1)} %copy-done.214), kind=kOutput, calls=%fused_computation.35 | convolution fusion | flops 6448742400 | bytes 17858560 | tf_op jit(solution)/shard_map/transpose(jvp(thm,shm->hts))/dot_general | solution.py:111
  969.0 20.1 %all-gather.19 = bf16[32,256]{1,0:T(8,128)(2,1)S(1)} all-gather(bf16[8,256]{1,0:T(8,128)(2,1)S(1)} %bitcast.1359), channel_id=21, replica_groups=mesh['section'=2,'dp'=4,'seq'=4] {'seq'}, dimensions={0}, use_global_device_ids=true | all-gather | bytes 20480 | tf_op jit(solution)/shard_map/all_gather | solution.py:36
  1012.4 10.5 fusion.451
  1032.0 16.7 %fusion.74 = (f32[512,8]{0,1:T(8,128)S(1)}, f32[8,512,256]{2,1,0:T(8,128)S(1)}) fusion(f32[8,256,512]{1,2,0:T(8,128)} %fusion.854, f32[8,512,256]{2,1,0:T(8,128)} %copy-done.16, f32[512]{0:T(512)S(1)} %copy-done.276, f32[8,256]{1,0:T(8,128)S(1)} %get-tuple-element.536, f32[512,8]{0,1:T(8,128)S(1)} %copy-done.214, f32[8,512,256]{2,1,0:T(8,128)} %copy-done.1, ...), kind=kOutput, calls=%fused_computation.112 | convolution fusion | flops 6456078336 | bytes 26290176 | tf_op jit(solution)/shard_map/transpose(jvp(thm,shm->hts))/dot_general | solution.py:111
  1141.5 40.2 %all-reduce.10 = (f32[512]{0:T(512)S(1)}, f32[512]{0:T(512)S(1)}) all-reduce(f32[512]{0:T(512)S(1)} %multiply_add_fusion.3, f32[512]{0:T(512)S(1)} %multiply_add_fusion.2), channel_id=28, replica_groups=mesh['section'=2,'dp'=4,'seq'=4] {'dp','seq'}, use_global_device_ids=true, to_apply=%region_117.118.clone | all-reduce | flops 1024 | bytes 8192
  1195.1 78.8 %reduce-scatter.9.cloned.1.call-done = f32[32,512]{1,0:T(8,128)} async-done(((f32[512,512]{1,0:T(8,128)}), f32[32,512]{1,0:T(8,128)}) %reduce-scatter.9.cloned.1.call-update) | async-done | bytes 65552 | tf_op jit(solution)/shard_map/reduce_scatter | solution.py:330
  1273.9 106.2 %reduce-scatter.17.cloned.1.call-done = f32[128,512]{1,0:T(8,128)} async-done(((f32[2048,512]{1,0:T(8,128)}), f32[128,512]{1,0:T(8,128)}) %reduce-scatter.17.cloned.1.call-update) | async-done | bytes 262160 | tf_op jit(solution)/shard_map/reduce_scatter | solution.py:330
  1380.1 97.4 %reduce-scatter.15.cloned.1.call-done = f32[32,2048]{1,0:T(8,128)} async-done(((f32[512,2048]{1,0:T(8,128)}), f32[32,2048]{1,0:T(8,128)}) %reduce-scatter.15.cloned.1.call-update) | async-done | bytes 262160 | tf_op jit(solution)/shard_map/reduce_scatter | solution.py:330
  (1071 shorter events, 638.2 us)
Async XLA Ops:
  7.2 148.7 %copy-start = (f32[1,8,64,256]{3,2,1,0:T(8,128)S(1)}, f32[1,8,64,256]{3,2,1,0:T(8,128)}, u32[]{:S(2)}) copy-start(f32[1,8,64,256]{3,2,1,0:T(8,128)} %param.27) | copy-start | bytes 1572868
  7.2 74.3 %copy-start.262 = (f32[1,32,512]{2,1,0:T(8,128)S(1)}, f32[1,32,512]{2,1,0:T(8,128)}, u32[]{:S(2)}) copy-start(f32[1,32,512]{2,1,0:T(8,128)} %param.29) | copy-start | bytes 196612
  7.2 250.8 %all-gather.29.cloned.1.call-start = ((), (), s32[]{:S(2)}) async-start(), calls=%async_computation.12 | async-start | bytes 1310720 | tf_op jit(solution)/shard_map/all_gather | solution.py:12
  13.8 104.3 %copy-start.146 = (bf16[1,1,512,512]{2,3,1,0:T(8,128)(2,1)}, bf16[1,1,512,512]{2,3,1,0:T(8,128)(2,1)S(1)}, u32[]{:S(2)}) copy-start(bf16[1,1,512,512]{2,3,1,0:T(8,128)(2,1)S(1)} %copy.427) | copy-start | bytes 1572868
  46.6 418.9 %copy-start.226 = (f32[512]{0:T(512)}, f32[512]{0:T(512)S(1)}, u32[]{:S(2)}) copy-start(f32[512]{0:T(512)S(1)} %convert_element_type.1084) | copy-start | bytes 6148
  153.9 216.8 %copy-start.67 = (bf16[1,512,512]{2,1,0:T(8,128)(2,1)}, bf16[1,512,512]{2,1,0:T(8,128)(2,1)S(1)}, u32[]{:S(2)}) copy-start(bf16[1,512,512]{2,1,0:T(8,128)(2,1)S(1)} %all-gather.1) | copy-start | bytes 1572868
  167.9 122.7 %all-gather.31.cloned.1.call-start = ((), (), s32[]{:S(2)}) async-start(), calls=%async_computation.13 | async-start | bytes 2228224 | tf_op jit(solution)/shard_map/all_gather | solution.py:255
  168.7 184.7 %all-gather.33.cloned.1.call-start = ((), (), s32[]{:S(2)}) async-start(), calls=%async_computation.14 | async-start | bytes 2228224 | tf_op jit(solution)/shard_map/all_gather | solution.py:255
  169.4 240.8 %all-gather.35.cloned.1.call-start = ((), (), s32[]{:S(2)}) async-start(), calls=%async_computation.15 | async-start | bytes 1310720 | tf_op jit(solution)/shard_map/all_gather | solution.py:12
  191.8 59.3 %copy-start.117 = (f32[512,512]{0,1:T(8,128)}, f32[512,512]{0,1:T(8,128)S(1)}, u32[]{:S(2)}) copy-start(f32[512,512]{0,1:T(8,128)S(1)} %fusion.524) | copy-start | bytes 3145732
  231.6 194.1 %copy-start.284 = (f32[512]{0:T(512)}, f32[512]{0:T(512)S(1)}, u32[]{:S(2)}) copy-start(f32[512]{0:T(512)S(1)} %compare_convert_fusion.10) | copy-start | bytes 6148
  288.4 73.4 %copy-start.204 = (bf16[1,1,512,512]{3,2,1,0:T(8,128)(2,1)S(1)}, bf16[1,1,512,512]{3,2,1,0:T(8,128)(2,1)}, u32[]{:S(2)}) copy-start(bf16[1,1,512,512]{3,2,1,0:T(8,128)(2,1)} %get-tuple-element.852) | copy-start | bytes 1572868
  360.1 5.4 collective-permute-start
  381.8 133.7 %all-gather.37.cloned.1.call-start = ((), (), s32[]{:S(2)}) async-start(), calls=%async_computation.16 | async-start | bytes 1310720 | tf_op jit(solution)/shard_map/all_gather | solution.py:12
  449.3 10.3 collective-permute-start.1
  481.2 144.2 %all-gather.39.cloned.1.call-start = ((), (), s32[]{:S(2)}) async-start(), calls=%async_computation.17 | async-start | bytes 1310720 | tf_op jit(solution)/shard_map/all_gather | solution.py:36
  577.8 282.4 %all-gather.41.cloned.1.call-start = ((), (), s32[]{:S(2)}) async-start(), calls=%async_computation.18 | async-start | bytes 1310720 | tf_op jit(solution)/shard_map/all_gather | solution.py:36
  682.4 82.9 %copy-start.83 = (f32[512,8,64]{0,2,1:T(8,128)}, f32[512,8,64]{0,2,1:T(8,128)S(1)}, u32[]{:S(2)}) copy-start(f32[512,8,64]{0,2,1:T(8,128)S(1)} %fusion.567) | copy-start | bytes 3145732
  686.7 94.3 %collective-permute-start.2 = (bf16[512,512]{0,1:T(8,128)(2,1)}, bf16[512,512]{0,1:T(8,128)(2,1)}, u32[]{:S(2)}, u32[]{:S(2)}) collective-permute-start(bf16[512,512]{0,1:T(8,128)(2,1)} %add_convert_fusion.4), channel_id=1, source_target_pairs={{16,0},{17,1},{18,2},{19,3},{20,4},{21,5},{22,6},{23,7},{24,8},{25... | collective-permute-start | bytes 1572872 | tf_op jit(solution)/shard_map/ppermute | solution.py:67
  704.7 87.2 %copy-start.8 = (f32[8,512,256]{2,1,0:T(8,128)}, f32[8,512,256]{2,1,0:T(8,128)S(1)}, u32[]{:S(2)}) copy-start(f32[8,512,256]{2,1,0:T(8,128)S(1)} %fusion.542) | copy-start | bytes 12582916
  704.8 139.0 %copy-start.210 = (f32[512,8]{0,1:T(8,128)}, f32[512,8]{0,1:T(8,128)S(1)}, u32[]{:S(2)}) copy-start(f32[512,8]{0,1:T(8,128)S(1)} %get-tuple-element.869) | copy-start | bytes 49156
  719.0 107.3 %copy-start.218 = (f32[512,8]{0,1:T(8,128)}, f32[512,8]{0,1:T(8,128)S(1)}, u32[]{:S(2)}) copy-start(f32[512,8]{0,1:T(8,128)S(1)} %get-tuple-element.867) | copy-start | bytes 49156
  728.9 114.9 %copy-start.222 = (f32[512,8]{0,1:T(8,128)}, f32[512,8]{0,1:T(8,128)S(1)}, u32[]{:S(2)}) copy-start(f32[512,8]{0,1:T(8,128)S(1)} %get-tuple-element.817) | copy-start | bytes 49156
  826.2 179.0 %all-gather.43.cloned.1.call-start = ((), (), s32[]{:S(2)}) async-start(), calls=%async_computation.19 | async-start | bytes 1310720 | tf_op jit(solution)/shard_map/all_gather | solution.py:36
  914.5 6.4 collective-permute-start.3
  928.6 60.4 %copy-start.89 = (f32[512,512]{0,1:T(8,128)}, f32[512,512]{0,1:T(8,128)S(1)}, u32[]{:S(2)}) copy-start(f32[512,512]{0,1:T(8,128)S(1)} %get-tuple-element.977) | copy-start | bytes 3145732
  934.8 250.8 %reduce-scatter.13.cloned.1.call-start = ((), (), s32[]{:S(2)}) async-start(), calls=%async_computation.9 | async-start | bytes 1114112 | tf_op jit(solution)/shard_map/reduce_scatter | solution.py:330
  964.2 221.4 %reduce-scatter.7.cloned.1.call-start = ((), (), s32[]{:S(2)}) async-start(), calls=%async_computation.6 | async-start | bytes 1114112 | tf_op jit(solution)/shard_map/reduce_scatter | solution.py:330
  1005.1 190.0 %reduce-scatter.11.cloned.1.call-start = ((), (), s32[]{:S(2)}) async-start(), calls=%async_computation.8 | async-start | bytes 1114112 | tf_op jit(solution)/shard_map/reduce_scatter | solution.py:330
  1031.9 242.0 %reduce-scatter.9.cloned.1.call-start = ((), (), s32[]{:S(2)}) async-start(), calls=%async_computation.7 | async-start | bytes 1114112 | tf_op jit(solution)/shard_map/reduce_scatter | solution.py:330
  1056.8 323.3 %reduce-scatter.17.cloned.1.call-start = ((), (), s32[]{:S(2)}) async-start(), calls=%async_computation.11 | async-start | bytes 4456448 | tf_op jit(solution)/shard_map/reduce_scatter | solution.py:330
  1068.6 408.9 %reduce-scatter.15.cloned.1.call-start = ((), (), s32[]{:S(2)}) async-start(), calls=%async_computation.10 | async-start | bytes 4456448 | tf_op jit(solution)/shard_map/reduce_scatter | solution.py:330
  (310 other events, 2922.1 us)
Sparse Core Ops, SparseCore 0:
  168.0 59.9 all-gather.28
  230.9 59.6 all-gather.30
  294.0 59.3 all-gather.32
  381.9 28.2 all-gather.34
  481.3 32.0 all-gather.36
  577.9 35.1 all-gather.38
  826.3 28.0 all-gather.40
  934.9 35.8 all-gather.42
  973.7 65.0 reduce-scatter.12
  1041.6 75.2 reduce-scatter.6
  1119.8 75.3 reduce-scatter.10
  1197.9 75.9 reduce-scatter.8
  1276.8 103.2 reduce-scatter.16
  1382.8 94.6 reduce-scatter.14
where the time goes:
time: 1490 us; the launch traced here: 1480 us
  matrix products  630 us (42%)
  waiting for transfers between devices  357 us (24%)
  blocking collectives  297 us (20%)
  local copies, waits for them, and re-layouts  84.2 us (6%)
  other arithmetic  61.8 us (4%)
  between operations  24.3 us (2%)
  starting transfers between devices  22.4 us (2%)
    reduce_scatter x6, waiting for transfers between devices, local(): lax.psum_scatter(totals, ('dp', 'seq'), scatter_dimension=0, tiled=True)  292 us
    dot_general x12, matrix products, attend(): jnp.einsum('thm,shm->hts', query_features, feats_k, precision=HIGH_PRECIS...  159 us
    all_gather x4, blocking collectives, local(): lax.all_gather(as_sent(lowered), ('dp', 'seq'), axis=0, tiled=True)  142 us
    dot_general x66, matrix products, matmul(): return jnp.dot(left, right, preferred_element_type=jnp.float32)  116 us
    dot_general x12, matrix products, attend(): jnp.einsum('hts,shd->thd', scores, value_heads, precision=HIGH_PRECISION)  103 us
    dot_general x18, matrix products, lift(): jnp.einsum('nhd,hdm->nhm', scaled, projection, precision=HIGH_PRECISION)  89.9 us
    unnamed x3, blocking collectives  76.7 us
    dot_general x12, matrix products, attend(): jnp.einsum('kec,ecz->kez', query_features, incoming_state, precision=HIGH...  66.9 us
  transfers between devices with their start and end apart: 18, of which 6 were waited for; matrix products, arithmetic and copies ran while one was open for 29% of the time, Pallas kernels for 0%

commit v1 on v0

--- a/solution.py
+++ b/solution.py
@@ -1,7 +1,958 @@
+import functools
+
 import jax
 import jax.numpy as jnp
 from jax import lax
+from jax.experimental import pallas as pl
+from jax.experimental.pallas import tpu as pltpu
 from jax.sharding import PartitionSpec as P
+
+MESH = pl.DeviceIdType.MESH
+F32 = jnp.float32
+BF16 = jnp.bfloat16
+VMEM_LIMIT = 63 << 20
+
+ROW_Q, ROW_K, ROW_V, ROW_O, ROW_UP, ROW_DOWN, SLAB = 32, 64, 96, 128, 160, 288, 416
+PORTIONS = ((0, 64), (128, 144))
+
+
+def dot(a, b):
+    return lax.dot_general(a, b, (((1,), (0,)), ((), ())), preferred_element_type=F32)
+
+
+def dot_nt(a, b):
+    return lax.dot_general(a, b, (((1,), (1,)), ((), ())), preferred_element_type=F32)
+
+
+def dot_tn(a, b):
+    return lax.dot_general(a, b, (((0,), (0,)), ((), ())), preferred_element_type=F32)
+
+
+def remote(src, dst, ssem, rsem, dev):
+    return pltpu.make_async_remote_copy(
+        src_ref=src, dst_ref=dst, send_sem=ssem, recv_sem=rsem, device_id=dev, device_id_type=MESH
+    )
+
+
+class Place:
+    def __init__(self):
+        self.c = lax.axis_index("section")
+        self.d = lax.axis_index("dp")
+        self.z = lax.axis_index("seq")
+        self.o = 1 - self.c
+        self.xn = self.d + 1 - 2 * lax.rem(self.d, 2)
+        self.yn = lax.rem(self.d + 2, 4)
+        self.first = self.xn + self.c * (self.yn - self.xn)
+        self.second = self.yn + self.c * (self.xn - self.yn)
+        self.diag = 3 - self.d
+        self.me = self.d * 4 + self.z
+
+    def at(self, d, z):
+        return (self.c, d, z)
+
+    def sibling(self):
+        return (self.o, self.d, self.z)
+
+    def peers(self):
+        out = [self.sibling(), self.at(self.xn, self.z), self.at(self.yn, self.z)]
+        return out + [self.at(self.d, lax.rem(self.z + k, 4)) for k in (1, 2, 3)]
+
+    def barrier(self):
+        bar = pltpu.get_barrier_semaphore()
+        peers = self.peers()
+        for dev in peers:
+            pl.semaphore_signal(bar, inc=1, device_id=dev, device_id_type=MESH)
+        pl.semaphore_wait(bar, len(peers))
+
+
+def weight(G, l, row, n=32):
+    return G[l, :, row : row + n, :].reshape(16 * n, 512)
+
+
+class Gather:
+    def __init__(self, pc, G, l, por, ssem, rsem, dsend, drecv):
+        base, self.n = PORTIONS[por]
+        self.pc, self.G, self.l, self.por = pc, G, l, por
+        self.sems = ssem, rsem, dsend, drecv
+        self.start = pl.multiple_of(base + pc.c * self.n, 16)
+        self.other = pl.multiple_of(base + pc.o * self.n, 16)
+
+    def ref(self, g):
+        return self.G.at[self.l, g, pl.ds(self.start, self.n)]
+
+    def link(self, g, i, dev):
+        ssem, rsem, _, _ = self.sems
+        return remote(self.ref(g), self.ref(g), ssem.at[self.l, self.por, i], rsem.at[self.l, self.por, g], dev)
+
+    def sib(self, g):
+        _, _, dsend, drecv = self.sems
+        return remote(
+            self.ref(g), self.ref(g), dsend.at[self.l, self.por, g], drecv.at[self.l, self.por, g], self.pc.sibling()
+        )
+
+    def arrive(self, g):
+        self.link(g, 0, self.pc.sibling()).wait_recv()
+
+    def own(self):
+        pc = self.pc
+        for k in (2, 1, 3):
+            self.link(pc.me, k, pc.at(pc.d, lax.rem(pc.z + k, 4))).start()
+        self.link(pc.me, 4, pc.at(pc.first, pc.z)).start()
+        self.link(pc.me, 8, pc.at(pc.second, pc.z)).start()
+
+    def column(self, k):
+        pc = self.pc
+
+        def step():
+            g = pc.d * 4 + lax.rem(pc.z + k, 4)
+            self.arrive(g)
+            self.link(g, 4 + k, pc.at(pc.first, pc.z)).start()
+            self.link(g, 8 + k, pc.at(pc.second, pc.z)).start()
+            self.sib(g).start()
+
+        if not isinstance(k, int):
+            pl.when(k > 0)(step)
+        elif k > 0:
+            step()
+
+    def across(self, k):
+        pc = self.pc
+        g = pc.first * 4 + lax.rem(pc.z + k, 4)
+        self.arrive(g)
+        self.link(g, 12 + k, pc.at(pc.second, pc.z)).start()
+        self.sib(g).start()
+
+    def far(self, k):
+        pc = self.pc
+        zz = lax.rem(pc.z + k, 4)
+        for dp in (pc.second, pc.diag):
+            g = dp * 4 + zz
+            self.arrive(g)
+            self.sib(g).start()
+
+    def finish(self):
+        _, _, dsend, drecv = self.sems
+        pc = self.pc
+
+        def wait(g):
+            ref = self.G.at[self.l, g, pl.ds(self.other, self.n)]
+            remote(ref, ref, dsend.at[self.l, self.por, g], drecv.at[self.l, self.por, g], pc.sibling()).wait_recv()
+
+        def step(i, _):
+            wait(lax.rem(pc.me + 1 + i, 16))
+            return 0
+
+        lax.fori_loop(0, 15, step, 0)
+
+    def drain(self):
+        pc = self.pc
+
+        def step(i, _):
+            self.link(pc.me, 1 + i, pc.at(pc.first, pc.z)).wait_send()
+            self.sib(lax.rem(pc.me + 1 + i, 16)).wait_send()
+            return 0
+
+        lax.fori_loop(0, 15, step, 0)
+
+
+def last_start(lengths, c, first_row, pos):
+    starts = []
+    at = 0
+    for i in range(3):
+        at = at + lengths[c, 0, i]
+        starts.append(at - first_row)
+    out = jnp.full(pos.shape, -first_row, jnp.int32)
+    for s in starts:
+        out = jnp.where(pos >= s, s, out)
+    return out, starts
+
+
+def norm(x):
+    c = x - jnp.mean(x, axis=-1, keepdims=True)
+    rstd = lax.rsqrt(jnp.mean(c * c, axis=-1, keepdims=True) + 1e-05)
+    return c * rstd, rstd
+
+
+def lane_low(shape):
+    return lax.rem(lax.broadcasted_iota(jnp.int32, shape, 1), 128) < 64
+
+
+def lift_pair(w, proj):
+    hi = w.astype(BF16)
+    low = (w - hi.astype(F32)).astype(BF16)
+    sq = (w * w).astype(BF16)
+    e = dot(jnp.concatenate([hi, sq, low, hi], axis=1), proj)
+    return (jnp.exp(e) * 0.0625).astype(BF16)
+
+
+def forward_kernel(
+    inputs, lengths, wq_in, wk_in, wv_in, wo_in, wup_in, wdown_in, gains_in, proj,
+    act, G_out, fq_out, fk_out, v_out, att_out, rden_out, branch_out, w_out, x_out, sin_out, pb_out,
+    G, px, pk, mask, xbuf, hbuf, qbuf, kbuf, fq, fk, vext, att, rden, branch, wqk, xin, sin, tail, sbuf,
+    gains, ybuf, hf, acc,
+    ssem, rsem, dsend, drecv, osem, osem2, psem, csend, crecv, asem, wsem,
+):
+    pc = Place()
+    c, z = pc.c, pc.z
+    G[c, pc.me, 0:ROW_Q, :] = gains_in[...]
+    for ref, row in ((wq_in, ROW_Q), (wk_in, ROW_K), (wv_in, ROW_V), (wo_in, ROW_O)):
+        G[c, pc.me, row : row + 32, :] = ref[0].astype(BF16)
+    for j in range(4):
+        row = ROW_UP + 32 * j
+        G[c, pc.me, row : row + 32, :] = wup_in[0, :, 512 * j : 512 * j + 512].astype(BF16)
+    G[c, pc.me, ROW_DOWN:SLAB, :] = wdown_in[0].astype(BF16)
+    hi = proj[0].astype(BF16)
+    px[c, 0] = hi
+    px[c, 1] = (proj[0] - hi.astype(F32)).astype(BF16)
+    pc.barrier()
+    halves = {}
+    for por, (base, n) in enumerate(PORTIONS):
+        for half, at in ((0, pc.o), (1, c)):
+            ref = G.at[c, pc.me, pl.ds(pl.multiple_of(base + at * n, 16), n)]
+            halves[por, half] = remote(ref, ref, osem2.at[0, por, half], osem2.at[1, por, half], pc.sibling())
+            halves[por, half].start()
+    psend = remote(px.at[c], px.at[c], psem.at[0], psem.at[1], pc.sibling())
+    psend.start()
+    moves = {
+        (l, por): Gather(pc, G, l, por, ssem, rsem, dsend, drecv) for l in (0, 1) for por in range(2)
+    }
+
+    def four(step):
+        for k in range(4):
+            step(k)
+
+    for por in (0, 1):
+        for half in (0, 1):
+            halves[por, half].wait()
+    moves[0, 0].own()
+
+    first_row = z * 512
+    rows = lax.broadcasted_iota(jnp.int32, (512, 512), 0)
+    cols = lax.broadcasted_iota(jnp.int32, (512, 512), 1)
+    begin, starts = last_start(lengths, c, first_row, rows)
+    mask[...] = ((cols <= rows) & (cols >= begin)).astype(F32)
+    prow = lax.broadcasted_iota(jnp.int32, (512, 1), 0)
+    begin_col, _ = last_start(lengths, c, first_row, prow)
+    head_mask = (begin_col < 0).astype(F32)
+    lane = lax.broadcasted_iota(jnp.int32, (1, 512), 1)
+    inner = [jnp.where((s < 512) & (s >= 0), s, 0) for s in starts]
+    cut = jnp.maximum(jnp.maximum(inner[0], inner[1]), inner[2])
+    tail_mask = (lane >= cut).astype(F32)
+
+    moves[0, 1].own()
+    psend.wait()
+    pk[...] = jnp.zeros_like(pk)
+    for l in (0, 1):
+        for p in range(4):
+            for h in (0, 1):
+                at = slice(64 * h, 64 * h + 64)
+                to = slice(256 * h, 256 * h + 256)
+                pk[l, p, at, to] = px[l, 0, 2 * p + h]
+                pk[l, p, 128 + 64 * h : 192 + 64 * h, to] = jnp.full((64, 256), -0.5, BF16)
+                pk[l, p, 256 + 64 * h : 320 + 64 * h, to] = px[l, 0, 2 * p + h]
+                pk[l, p, 384 + 64 * h : 448 + 64 * h, to] = px[l, 1, 2 * p + h]
+    vext[:, :, :, 128:] = jnp.ones((2, 4, 512, 128), BF16)
+
+    @pl.when(z == 0)
+    def _():
+        sin[...] = jnp.zeros_like(sin)
+
+    xbuf[...] = inputs[c, 0].astype(F32)
+    four(moves[0, 0].column)
+    moves[1, 0].own()
+    four(moves[0, 0].across)
+    moves[1, 1].own()
+    four(moves[0, 1].column)
+    four(moves[0, 0].far)
+    four(moves[0, 1].across)
+    moves[0, 0].finish()
+    below = (c, pc.d, jnp.minimum(z + 1, 3))
+    low = lane_low((512, 128))
+    row_low = lax.broadcasted_iota(jnp.int32, (144, 256), 0)
+    tail_is_first = (row_low < 64) | ((row_low >= 128) & (row_low < 136))
+    low256 = lane_low((256, 128))
+
+    def chain(l, p):
+        return remote(sbuf.at[l, p], sin.at[l, p], csend.at[l, p], crecv.at[l, p], below)
+
+    def layer(l, during):
+        gains[...] = jnp.sum(G[l, :, 0:16, :].astype(F32), axis=0)
+
+        def norm_tile(i, _):
+            at = pl.ds(pl.multiple_of(i * 128, 128), 128)
+            x = xbuf[at, :]
+            xin[l, at, :] = x.astype(BF16)
+            hbuf[at, :] = (norm(x)[0] * gains[0:1, :]).astype(BF16)
+            return 0
+
+        lax.fori_loop(0, 4, norm_tile, 0)
+        scale = 64 ** (-0.25)
+        kbuf[...] = dot(hbuf[...], weight(G, l, ROW_K)) * scale
+        qbuf[...] = dot(hbuf[...], weight(G, l, ROW_V))
+
+        def key_pair(p, _):
+            if "key" in during:
+                during["key"](p)
+            at = pl.ds(pl.multiple_of(p * 128, 128), 128)
+            w = kbuf[:, at]
+            wqk[l, 1, p] = w.astype(BF16)
+            f = lift_pair(w, pk[l, p])
+            fk[l, p] = f
+            v = qbuf[:, at]
+            vext[l, p, :, 0:128] = v.astype(BF16)
+            vt = jnp.concatenate([v.T * tail_mask, jnp.broadcast_to(tail_mask, (16, 512))], axis=0).astype(BF16)
+            t = jnp.where(tail_is_first, dot(vt, f[:, 0:256]), dot(vt, f[:, 256:512]))
+            tail[p] = t
+
+            @pl.when(z == 0)
+            def _():
+                sbuf[l, p] = t.astype(BF16)
+                chain(l, p).start()
+
+            return 0
+
+        lax.fori_loop(0, 4, key_pair, 0)
+        qbuf[...] = dot(hbuf[...], weight(G, l, ROW_Q)) * scale
+
+        def query_pair(p, _):
+            if "query" in during:
+                during["query"](p)
+            at = pl.ds(pl.multiple_of(p * 128, 128), 128)
+            w = qbuf[:, at]
+            wqk[l, 0, p] = w.astype(BF16)
+            fq[l, p] = lift_pair(w, pk[l, p])
+            return 0
+
+        lax.fori_loop(0, 4, query_pair, 0)
+
+        def attend_pair(p, _):
+            if "attend" in during:
+                during["attend"](p)
+            at = pl.ds(pl.multiple_of(p * 128, 128), 128)
+
+            @pl.when(z > 0)
+            def _():
+                chain(l, p).wait_recv()
+
+            @pl.when((z > 0) & (z < 3))
+            def _():
+                sbuf[l, p] = (tail[p] + sin[l, p].astype(F32)).astype(BF16)
+                chain(l, p).start()
+
+            for t in (0, 1):
+                n = 256 * (t + 1)
+                tr = slice(256 * t, 256 * t + 256)
+                res = []
+                for h in (0, 1):
+                    fl = slice(256 * h, 256 * h + 256)
+                    fqh = fq[l, p, tr, fl]
+                    a = (dot_nt(fqh, fk[l, p, 0:n, fl]) * mask[tr, 0:n]).astype(BF16)
+                    zrow = sin[l, p, 128:144, :].astype(F32)[8 * h : 8 * h + 1, :]
+                    st = jnp.concatenate(
+                        [sin[l, p, 0:128, :], jnp.broadcast_to(zrow, (128, 256)).astype(BF16)], axis=0
+                    )
+                    res.append(dot(a, vext[l, p, 0:n, :]) + head_mask[tr, :] * dot_nt(fqh, st))
+                num = jnp.where(low256, res[0][:, 0:128], res[1][:, 0:128])
+                den = jnp.where(low256, res[0][:, 128:256], res[1][:, 128:256])
+                r = 1.0 / den
+                att[l, tr, at] = num * r
+                rden[l, tr, at] = r
+            return 0
+
+        lax.fori_loop(0, 4, attend_pair, 0)
+
+        if "branch" in during:
+            during["branch"]()
+
+        def branch_tile(i, _):
+            at = pl.ds(pl.multiple_of(i * 256, 256), 256)
+            b = xbuf[at, :] + dot(att[l, at, :].astype(BF16), weight(G, l, ROW_O))
+            branch[l, at, :] = b
+            hf[at, :] = (norm(b)[0] * gains[1:2, :]).astype(BF16)
+            acc[at, :] = b
+            return 0
+
+        lax.fori_loop(0, 2, branch_tile, 0)
+
+        def ffn_tile(j, _):
+            if "ffn" in during:
+                during["ffn"](j)
+            up = G[l, :, pl.ds(pl.multiple_of(ROW_UP + 32 * j, 32), 32), :].reshape(512, 512)
+            down = G[l, pl.ds(4 * j, 4), ROW_DOWN:SLAB, :].reshape(512, 512)
+            for i in (0, 1):
+                at = slice(256 * i, 256 * i + 256)
+                pre = dot(hf[at, :], up)
+                hid = jax.nn.gelu(pre).astype(BF16)
+                acc[at, :] += dot(hid, down)
+            return 0
+
+        lax.fori_loop(0, 4, ffn_tile, 0)
+        y = acc[...].astype(BF16)
+        ybuf[l] = y
+        xbuf[...] = y.astype(F32)
+        for i, (src, dst) in enumerate(saved):
+            pltpu.make_async_copy(src.at[l], dst.at[l], wsem.at[l, i]).start()
+
+    saved = (
+        (G, G_out), (fq, fq_out), (fk, fk_out), (vext, v_out), (att, att_out), (rden, rden_out),
+        (branch, branch_out), (wqk, w_out), (xin, x_out), (sin, sin_out),
+    )
+
+    def before_branch(l):
+        if l == 0:
+            four(moves[0, 1].far)
+        moves[l, 1].finish()
+
+    layer(0, {"key": moves[1, 0].column, "query": moves[1, 1].column, "attend": moves[1, 0].across,
+              "branch": lambda: before_branch(0), "ffn": moves[1, 1].across})
+    four(moves[1, 0].far)
+    moves[1, 0].finish()
+    layer(1, {"query": moves[1, 1].far, "branch": lambda: before_branch(1)})
+    keep = pltpu.make_async_copy(pk.at[:, :, 0:256, :], pb_out, osem)
+    keep.start()
+    own_act = pltpu.make_async_copy(ybuf.at[c], act.at[c], asem.at[0])
+    own_act.start()
+    far_act = remote(ybuf.at[pc.o], act.at[c], asem.at[1], asem.at[2], pc.sibling())
+    far_act.start()
+    own_act.wait()
+    far_act.wait()
+    keep.wait()
+    for l in (0, 1):
+        for i, (src, dst) in enumerate(saved):
+            pltpu.make_async_copy(src.at[l], dst.at[l], wsem.at[l, i]).wait()
+
+    @pl.when(z < 3)
+    def _():
+        for l in (0, 1):
+            for p in range(4):
+                chain(l, p).wait_send()
+
+    for move in moves.values():
+        move.drain()
+
+
+def forward_call(inputs, lengths, weights, gain_rows, proj):
+    sds = jax.ShapeDtypeStruct
+    dma = pltpu.SemaphoreType.DMA
+    vm = pl.BlockSpec(memory_space=pltpu.VMEM)
+    hbm = pl.BlockSpec(memory_space=pl.ANY)
+    saved = [
+        sds((2, 16, SLAB, 512), BF16), sds((2, 4, 512, 512), BF16), sds((2, 4, 512, 512), BF16),
+        sds((2, 4, 512, 256), BF16), sds((2, 512, 512), F32), sds((2, 512, 512), F32), sds((2, 512, 512), F32),
+        sds((2, 2, 4, 512, 128), BF16), sds((2, 512, 512), BF16), sds((2, 4, 144, 256), BF16),
+        sds((2, 4, 256, 512), BF16),
+    ]
+    scratch = [
+        pltpu.VMEM((2, 16, SLAB, 512), BF16),
+        pltpu.VMEM((2, 2, 8, 64, 256), BF16),
+        pltpu.VMEM((2, 4, 512, 512), BF16),
+        pltpu.VMEM((512, 512), F32),
+        pltpu.VMEM((512, 512), F32),
+        pltpu.VMEM((512, 512), BF16),
+        pltpu.VMEM((512, 512), F32),
+        pltpu.VMEM((512, 512), F32),
+        pltpu.VMEM((2, 4, 512, 512), BF16),
+        pltpu.VMEM((2, 4, 512, 512), BF16),
+        pltpu.VMEM((2, 4, 512, 256), BF16),
+        pltpu.VMEM((2, 512, 512), F32),
+        pltpu.VMEM((2, 512, 512), F32),
+        pltpu.VMEM((2, 512, 512), F32),
+        pltpu.VMEM((2, 2, 4, 512, 128), BF16),
+        pltpu.VMEM((2, 512, 512), BF16),
+        pltpu.VMEM((2, 4, 144, 256), BF16),
+        pltpu.VMEM((4, 144, 256), F32),
+        pltpu.VMEM((2, 4, 144, 256), BF16),
+        pltpu.VMEM((16, 512), F32),
+        pltpu.VMEM((2, 512, 512), BF16),
+        pltpu.VMEM((512, 512), BF16),
+        pltpu.VMEM((512, 512), F32),
+        dma((2, 2, 16)), dma((2, 2, 16)), dma((2, 2, 16)), dma((2, 2, 16)), dma, dma((2, 2, 2)), dma((2,)),
+        dma((2, 4)), dma((2, 4)), dma((3,)), dma((2, 10)),
+    ]
+    return pl.pallas_call(
+        forward_kernel,
+        out_shape=[sds((2, 512, 512), BF16)] + saved,
+        in_specs=[vm, pl.BlockSpec(memory_space=pltpu.SMEM)] + [vm] * 8,
+        out_specs=[vm] + [hbm] * len(saved),
+        scratch_shapes=scratch,
+        compiler_params=pltpu.CompilerParams(
+            collective_id=0, has_side_effects=True, vmem_limit_bytes=VMEM_LIMIT
+        ),
+        name="forward",
+    )(inputs, lengths, *weights, gain_rows, proj)
+
+
+def make_gain_rows(gain_attn, gain_ffn):
+    g = lax.axis_index("dp") * 4 + lax.axis_index("seq")
+    lane = lax.broadcasted_iota(jnp.int32, (1, 512), 1)
+    mine = lane // 32 == g
+
+    def gain_row(gain):
+        return jnp.where(mine, jnp.tile(gain[None, :].astype(BF16), (1, 16)), jnp.zeros((), BF16))
+
+    return jnp.concatenate([gain_row(gain_attn), gain_row(gain_ffn), jnp.zeros((30, 512), BF16)], axis=0)
+
+
+def gelu_parts(x):
+    k = 0.7978845608028654
+    x2 = x * x
+    t = jnp.tanh(k * x * (1.0 + 0.044715 * x2))
+    half = 0.5 * (1.0 + t)
+    return x * half, half + 0.5 * x * (1.0 - t * t) * k * (1.0 + 0.134145 * x2)
+
+
+def norm_back(y, rstd, dy):
+    m1 = jnp.mean(dy, axis=-1, keepdims=True)
+    m2 = jnp.mean(dy * y, axis=-1, keepdims=True)
+    return rstd * (dy - m1 - y * m2)
+
+
+HALF = SLAB // 2
+SUM_PORTIONS = ((ROW_UP, 128), (0, 80))
+
+
+class Sums:
+    def __init__(self, pc, slabs, bufs, sems, l, por):
+        base, self.n = SUM_PORTIONS[por]
+        self.pc, self.slabs, self.l, self.por = pc, slabs, l, por
+        self.sb, self.r1, self.r2, self.r3, self.keep = bufs
+        self.sems = sems
+        self.mine = pl.multiple_of(base + pc.c * self.n, 16)
+        self.other = pl.multiple_of(base + pc.o * self.n, 16)
+        self.at = pl.ds(sum(2 * n for _, n in SUM_PORTIONS[:por]) // 2, self.n)
+
+    def copy(self, i, j, src, dst, dev):
+        ssem, rsem = self.sems
+        return remote(src, dst, ssem.at[self.l, self.por, i, j], rsem.at[self.l, self.por, i, j], dev)
+
+    def to_sibling(self, g):
+        src = self.slabs.at[self.l, g, pl.ds(self.other, self.n)]
+        return self.copy(0, g, src, self.sb.at[self.l, g, self.at], self.pc.sibling())
+
+    def to_second(self, j, zz, g):
+        src, dst = self.sb.at[self.l, g, self.at], self.r1.at[self.l, j, zz, self.at]
+        return self.copy(1, 4 * j + zz, src, dst, self.pc.at(self.pc.second, self.pc.z))
+
+    def to_first(self, zz, g):
+        src, dst = self.sb.at[self.l, g, self.at], self.r2.at[self.l, zz, self.at]
+        return self.copy(2, zz, src, dst, self.pc.at(self.pc.first, self.pc.z))
+
+    def along(self, k, g):
+        src, dst = self.sb.at[self.l, g, self.at], self.r3.at[self.l, 3 - k, self.at]
+        return self.copy(3, 3 - k, src, dst, self.pc.at(self.pc.d, lax.rem(self.pc.z + k, 4)))
+
+    def begin(self):
+        pc = self.pc
+        for col in (pc.diag, pc.second, pc.first, pc.d):
+            for k in (1, 2, 3, 0):
+                self.to_sibling(col * 4 + lax.rem(pc.z + k, 4)).start()
+
+    def pair(self, g):
+        self.to_sibling(g).wait_recv()
+        own = self.slabs[self.l, g, pl.ds(self.mine, self.n), :]
+        return own.astype(F32) + self.sb[self.l, g, self.at, :].astype(F32)
+
+    def stage1(self, j, i):
+        pc = self.pc
+        zz = lax.rem(pc.z + 1 + i, 4)
+        g = (pc.diag if j == 0 else pc.second) * 4 + zz
+        self.sb[self.l, g, self.at, :] = self.pair(g).astype(BF16)
+        self.to_second(j, zz, g).start()
+
+    def stage2(self, i):
+        pc = self.pc
+        zz = lax.rem(pc.z + 1 + i, 4)
+        g = pc.first * 4 + zz
+        s = self.pair(g)
+        self.to_second(0, zz, g).wait_recv()
+        self.sb[self.l, g, self.at, :] = (s + self.r1[self.l, 0, zz, self.at, :].astype(F32)).astype(BF16)
+        self.to_first(zz, g).start()
+
+    def stage3(self, k):
+        pc = self.pc
+        zz = lax.rem(pc.z + k, 4)
+        g = pc.d * 4 + zz
+        s = self.pair(g)
+        self.to_second(1, zz, g).wait_recv()
+        s = s + self.r1[self.l, 1, zz, self.at, :].astype(F32)
+        self.to_first(zz, g).wait_recv()
+        s = s + self.r2[self.l, zz, self.at, :].astype(F32)
+        if k:
+            self.sb[self.l, g, self.at, :] = s.astype(BF16)
+            self.along(k, g).start()
+        else:
+            self.keep[self.l, self.at, :] = s
+
+    def stage4(self, l):
+        s = self.keep[l, self.at, :]
+        for i in range(3):
+            s = s + self.r3[l, i, self.at, :].astype(F32)
+        return s
+
+    def arrive(self):
+        for k in (1, 2, 3):
+            self.along(k, self.pc.me).wait_recv()
+
+    def drain(self):
+        for i in range(16):
+            self.to_sibling(i).wait_send()
+        for j in (0, 1):
+            for zz in range(4):
+                self.to_second(j, zz, 0).wait_send()
+        for zz in range(4):
+            self.to_first(zz, 0).wait_send()
+        for k in (1, 2, 3):
+            self.along(k, 0).wait_send()
+
+
+def backward_kernel(
+    cotangent, lengths, G_in, fq_in, fk_in, v_in, att_in, rden_in, branch_in, w_in, x_in, sin_in, pb_in,
+    gin, gq_out, gk_out, gv_out, go_out, gup_out, gdown_out, gg_out,
+    G, fq, fk, vext, att, rden, branch, wqk, xin, sin, pb,
+    mask, mask_t, gbuf, gbr, hbuf, hT, gb, dh, gq, gk, gv, le, rin, rtail, rbuf, gains, gsum, xout, slabs,
+    sb, r1, r2, r3, keep, total,
+    lsem, csend, crecv, asem, ssem, rsem, fsem,
+):
+    pc = Place()
+    c, z = pc.c, pc.z
+    loads = (
+        (G_in, G), (fq_in, fq), (fk_in, fk), (v_in, vext), (att_in, att), (rden_in, rden), (branch_in, branch),
+        (w_in, wqk), (x_in, xin), (sin_in, sin), (pb_in, pb),
+    )
+
+    def load(l, i):
+        src, dst = loads[i]
+        return pltpu.make_async_copy(src.at[l], dst, lsem.at[i])
+
+    pc.barrier()
+    for i in range(len(loads)):
+        load(1, i).start()
+
+    first_row = z * 512
+    rows = lax.broadcasted_iota(jnp.int32, (512, 512), 0)
+    cols = lax.broadcasted_iota(jnp.int32, (512, 512), 1)
+    begin, starts = last_start(lengths, c, first_row, rows)
+    mask[...] = ((cols <= rows) & (cols >= begin)).astype(F32).astype(BF16)
+    begin, _ = last_start(lengths, c, first_row, cols)
+    mask_t[...] = ((rows <= cols) & (rows >= begin)).astype(F32).astype(BF16)
+    prow = lax.broadcasted_iota(jnp.int32, (512, 1), 0)
+    begin_col, _ = last_start(lengths, c, first_row, prow)
+    head_col = (begin_col < 0).astype(F32)
+    lane = lax.broadcasted_iota(jnp.int32, (1, 512), 1)
+    begin_row, _ = last_start(lengths, c, first_row, lane)
+    head_row = (begin_row < 0).astype(F32)
+    inner = [jnp.where((s < 512) & (s >= 0), s, 0) for s in starts]
+    cut = jnp.maximum(jnp.maximum(inner[0], inner[1]), inner[2])
+    tail_col = (prow >= cut).astype(F32)
+
+    @pl.when(z == 3)
+    def _():
+        rin[...] = jnp.zeros_like(rin)
+
+    gbuf[...] = cotangent[c, 0].astype(F32)
+    above = (c, pc.d, jnp.maximum(z - 1, 0))
+    row_low = lax.broadcasted_iota(jnp.int32, (144, 256), 0)
+    tail_is_first = (row_low < 64) | ((row_low >= 128) & (row_low < 136))
+    low = lane_low((512, 128))
+    ones_i = lax.broadcasted_iota(jnp.int32, (256, 128), 0)
+    ones_j = lax.broadcasted_iota(jnp.int32, (256, 128), 1)
+    head_ones = (lax.rem(ones_i, 128) // 64 == ones_j // 64).astype(BF16)
+    scale = 64 ** (-0.25)
+
+    def chain(l, p):
+        return remote(rbuf.at[l, p], rin.at[l, p], csend.at[l, p], crecv.at[l, p], above)
+
+    sums = {(l, por): Sums(pc, slabs, (sb, r1, r2, r3, keep), (ssem, rsem), l, por) for l in (0, 1) for por in (0, 1)}
+
+    def put(l, row, n, value):
+        slabs[l, :, row : row + n, :] = value.astype(BF16).reshape(16, n, 512)
+
+    def layer(l, during):
+        def at_point(name, *args):
+            if name in during:
+                during[name](*args)
+
+        for i in range(len(loads)):
+            load(l, i).wait()
+        gains[...] = jnp.sum(G[:, 0:16, :].astype(F32), axis=0)
+        gsum[...] = jnp.zeros_like(gsum)
+
+        def norm_tile(i, _):
+            at = pl.ds(pl.multiple_of(i * 128, 128), 128)
+            hbuf[at, :] = (norm(branch[at, :])[0] * gains[1:2, :]).astype(BF16)
+            gb[at, :] = gbuf[at, :].astype(BF16)
+            return 0
+
+        lax.fori_loop(0, 4, norm_tile, 0)
+        hT[...] = hbuf[...].T
+        dh[...] = jnp.zeros_like(dh)
+
+        def ffn_tile(j, _):
+            at_point("ffn", j)
+            up_at = pl.ds(pl.multiple_of(ROW_UP + 32 * j, 32), 32)
+            up = G[:, up_at, :].reshape(512, 512)
+            down = G[pl.ds(4 * j, 4), ROW_DOWN:SLAB, :].reshape(512, 512)
+            for i in (0, 1):
+                at = slice(256 * i, 256 * i + 256)
+                hid, slope = gelu_parts(dot(hbuf[at, :], up))
+                gq[at, :] = hid.astype(BF16)
+                gk[at, :] = (slope * dot_nt(gb[at, :], down)).astype(BF16)
+            slabs[l, pl.ds(4 * j, 4), ROW_DOWN:SLAB, :] = dot_tn(gq[...], gb[...]).astype(BF16).reshape(4, 128, 512)
+            g = gk[...]
+            slabs[l, :, up_at, :] = dot(hT[...], g).astype(BF16).reshape(16, 32, 512)
+            dh[...] += dot_nt(g, up)
+            return 0
+
+        lax.fori_loop(0, 4, ffn_tile, 0)
+
+        sums[l, 0].begin()
+
+        def branch_tile(i, _):
+            at_point("branch", i)
+            at = pl.ds(pl.multiple_of(i * 128, 128), 128)
+            y, rstd = norm(branch[at, :])
+            d = dh[at, :]
+            gsum[1:2, :] += jnp.sum(d * y, axis=0, keepdims=True)
+            g = gbuf[at, :] + norm_back(y, rstd, d * gains[1:2, :])
+            gbr[at, :] = g
+            gb[at, :] = g.astype(BF16)
+            hbuf[at, :] = att[at, :].astype(BF16)
+            return 0
+
+        lax.fori_loop(0, 4, branch_tile, 0)
+        put(l, ROW_O, 32, dot_tn(hbuf[...], gb[...]))
+        dh[...] = dot_nt(gb[...], G[:, ROW_O : ROW_O + 32, :].reshape(512, 512))
+
+        def tail_pair(p, _):
+            at_point("tail", p)
+            at = pl.ds(pl.multiple_of(p * 128, 128), 128)
+            g = dh[:, at]
+            r = rden[:, at]
+            t = g * att[:, at]
+            hi = t.astype(BF16)
+            lo = (t - hi.astype(F32)).astype(BF16)
+            dden = -dot(jnp.concatenate([hi, lo], axis=1), head_ones) * r
+            dnum = g * r
+            le[p] = jnp.concatenate([dnum, dden * (1.0 / 64.0)], axis=1).astype(BF16)
+            dt = (dden.T) * head_row
+            lhs = jnp.concatenate([dnum.T * head_row, dt[0:8], dt[64:72]], axis=0).astype(BF16)
+            tl = jnp.where(tail_is_first, dot(lhs, fq[p, :, 0:256]), dot(lhs, fq[p, :, 256:512]))
+            rtail[p] = tl
+
+            @pl.when(z == 3)
+            def _():
+                rbuf[l, p] = tl.astype(BF16)
+                chain(l, p).start()
+
+            return 0
+
+        lax.fori_loop(0, 4, tail_pair, 0)
+
+        def attend_pair(p, _):
+            at_point("attend", p)
+            at = pl.ds(pl.multiple_of(p * 128, 128), 128)
+
+            @pl.when(z < 3)
+            def _():
+                chain(l, p).wait_recv()
+
+            @pl.when((z > 0) & (z < 3))
+            def _():
+                rbuf[l, p] = (rtail[p] + rin[l, p].astype(F32)).astype(BF16)
+                chain(l, p).start()
+
+            ve = vext[p]
+            lep = le[p]
+            dq, dk, dv = [], [], []
+            for h in (0, 1):
+                fl = slice(256 * h, 256 * h + 256)
+                keep = lane_low((512, 256)) if h == 0 else jnp.logical_not(lane_low((512, 256)))
+                leh = jnp.where(keep, lep, jnp.zeros((), BF16))
+                fqh, fkh = fq[p, :, fl], fk[p, :, fl]
+                zrow = sin[p, 128:144, :].astype(F32)[8 * h : 8 * h + 1, :]
+                st = jnp.concatenate([sin[p, 0:128, :], jnp.broadcast_to(zrow, (128, 256)).astype(BF16)], axis=0)
+                rrow = rin[l, p, 128:144, :].astype(F32)[8 * h : 8 * h + 1, :] * (1.0 / 128.0)
+                rows_h = lax.broadcasted_iota(jnp.int32, (128, 256), 0) // 64 == h
+                rt = jnp.where(rows_h, rin[l, p, 0:128, :], jnp.zeros((), BF16))
+                rte = jnp.concatenate([rt, jnp.broadcast_to(rrow, (128, 256)).astype(BF16)], axis=0)
+                dqh = head_col * dot(leh, st)
+                da0 = dot_nt(leh[0:256], ve[0:256]).astype(BF16) * mask[0:256, 0:256]
+                da1 = dot_nt(leh[256:512], ve).astype(BF16) * mask[256:512, :]
+                dqh = dqh + jnp.concatenate([dot(da0, fkh[0:256]), dot(da1, fkh)], axis=0)
+                at0 = dot_nt(fkh[0:256], fqh).astype(BF16) * mask_t[0:256, :]
+                at1 = dot_nt(fkh[256:512], fqh[256:512]).astype(BF16) * mask_t[256:512, 256:512]
+                dvh = tail_col * dot_nt(fkh, rin[l, p, 0:128, :])
+                dvh = dvh + jnp.concatenate([dot(at0, lep[:, 0:128]), dot(at1, lep[256:512, 0:128])], axis=0)
+                dt0 = dot_nt(ve[0:256], leh).astype(BF16) * mask_t[0:256, :]
+                dt1 = dot_nt(ve[256:512], leh[256:512]).astype(BF16) * mask_t[256:512, 256:512]
+                dkh = tail_col * dot(ve, rte)
+                dkh = dkh + jnp.concatenate([dot(dt0, fqh), dot(dt1, fqh[256:512])], axis=0)
+                dq.append((dqh * fqh.astype(F32)).astype(BF16))
+                dk.append((dkh * fkh.astype(F32)).astype(BF16))
+                dv.append(dvh)
+            gv[:, at] = jnp.where(low, dv[0], dv[1]).astype(BF16)
+            for k, e, out in ((0, dq, gq), (1, dk, gk)):
+                gw = dot_nt(jnp.concatenate(e, axis=1), pb[p])
+                gw = gw[:, 0:128] + 2.0 * wqk[k, p].astype(F32) * gw[:, 128:256]
+                out[:, at] = (gw * scale).astype(BF16)
+            return 0
+
+        lax.fori_loop(0, 4, attend_pair, 0)
+
+        def norm_tile2(i, _):
+            at_point("norm", i)
+            at = pl.ds(pl.multiple_of(i * 128, 128), 128)
+            hbuf[at, :] = (norm(xin[at, :].astype(F32))[0] * gains[0:1, :]).astype(BF16)
+            return 0
+
+        lax.fori_loop(0, 4, norm_tile2, 0)
+        hT[...] = hbuf[...].T
+        for row, g in ((ROW_Q, gq), (ROW_K, gk), (ROW_V, gv)):
+            put(l, row, 32, dot(hT[...], g[...]))
+        dh[...] = dot_nt(gq[...], G[:, ROW_Q : ROW_Q + 32, :].reshape(512, 512))
+        dh[...] += dot_nt(gk[...], G[:, ROW_K : ROW_K + 32, :].reshape(512, 512))
+        dh[...] += dot_nt(gv[...], G[:, ROW_V : ROW_V + 32, :].reshape(512, 512))
+
+        def out_tile(i, _):
+            at_point("out", i)
+            at = pl.ds(pl.multiple_of(i * 128, 128), 128)
+            y, rstd = norm(xin[at, :].astype(F32))
+            d = dh[at, :]
+            gsum[0:1, :] += jnp.sum(d * y, axis=0, keepdims=True)
+            g = (gbr[at, :] + norm_back(y, rstd, d * gains[0:1, :])).astype(BF16)
+            xout[l, at, :] = g
+            gbuf[at, :] = g.astype(F32)
+            return 0
+
+        lax.fori_loop(0, 4, out_tile, 0)
+        slabs[l, :, 0:16, :] = jnp.broadcast_to(gsum[...].astype(BF16)[None], (16, 16, 512))
+        slabs[l, :, 16:32, :] = jnp.zeros((16, 16, 512), BF16)
+
+        sums[l, 1].begin()
+        if l == 1:
+            for i in range(len(loads)):
+                load(0, i).start()
+
+
+    def four(step, *args):
+        for i in range(4):
+            step(*args, i)
+
+    layer(1, {"tail": lambda p: sums[1, 0].stage1(0, p), "attend": lambda p: sums[1, 0].stage1(1, p),
+              "norm": sums[1, 0].stage2})
+    for k in (1, 2, 3, 0):
+        sums[1, 0].stage3(k)
+    layer(0, {"ffn": lambda p: (sums[1, 1].stage1(0, p), sums[1, 1].stage1(1, p)), "branch": sums[1, 1].stage2,
+              "tail": lambda p: sums[0, 0].stage1(0, p), "attend": lambda p: sums[0, 0].stage1(1, p),
+              "norm": sums[0, 0].stage2})
+    own_act = pltpu.make_async_copy(xout.at[c], gin.at[c], asem.at[0])
+    own_act.start()
+    far_act = remote(xout.at[pc.o], gin.at[c], asem.at[1], asem.at[2], pc.sibling())
+    far_act.start()
+    own_act.wait()
+    far_act.wait()
+
+    four(sums[0, 1].stage1, 0)
+    four(sums[0, 1].stage1, 1)
+    for k in (1, 2, 3, 0):
+        sums[1, 1].stage3(k)
+    for k in (1, 2, 3, 0):
+        sums[0, 0].stage3(k)
+    four(sums[0, 1].stage2)
+    for k in (1, 2, 3, 0):
+        sums[0, 1].stage3(k)
+    for m in sums.values():
+        m.arrive()
+    for por in (0, 1):
+        m = sums[0, por]
+        gbr[m.at, :] = m.stage4(pc.o)
+    parts = []
+    for por in (0, 1):
+        m = sums[0, por]
+        part = remote(gbr.at[m.at], total.at[pl.ds(m.mine, m.n)], fsem.at[0, por], fsem.at[1, por], pc.sibling())
+        part.start()
+        parts.append(part)
+    for por in (0, 1):
+        m = sums[0, por]
+        total[pl.ds(m.mine, m.n), :] = m.stage4(c)
+    for part in parts:
+        part.wait()
+    for ref, row in ((gq_out, ROW_Q), (gk_out, ROW_K), (gv_out, ROW_V), (go_out, ROW_O)):
+        ref[...] = total[row : row + 32, :]
+    for j in range(4):
+        gup_out[:, 512 * j : 512 * j + 512] = total[ROW_UP + 32 * j : ROW_UP + 32 * j + 32, :]
+    gdown_out[...] = total[ROW_DOWN:SLAB, :]
+    gg_out[...] = pltpu.roll(total[0:8, :], lax.rem(512 - 32 * pc.me, 512), 1)
+    for m in sums.values():
+        m.drain()
+
+    @pl.when(z > 0)
+    def _():
+        for l in (0, 1):
+            for p in range(4):
+                chain(l, p).wait_send()
+
+
+def backward_call(cotangent, lengths, saved):
+    sds = jax.ShapeDtypeStruct
+    dma = pltpu.SemaphoreType.DMA
+    vm = pl.BlockSpec(memory_space=pltpu.VMEM)
+    hbm = pl.BlockSpec(memory_space=pl.ANY)
+    bufs = [pltpu.VMEM(a.shape[1:], a.dtype) for a in saved]
+    full = (512, 512)
+    scratch = bufs + [
+        pltpu.VMEM(full, BF16),
+        pltpu.VMEM(full, BF16),
+        pltpu.VMEM(full, F32),
+        pltpu.VMEM(full, F32),
+        pltpu.VMEM(full, BF16),
+        pltpu.VMEM(full, BF16),
+        pltpu.VMEM(full, BF16),
+        pltpu.VMEM(full, F32),
+        pltpu.VMEM(full, BF16),
+        pltpu.VMEM(full, BF16),
+        pltpu.VMEM(full, BF16),
+        pltpu.VMEM((4, 512, 256), BF16),
+        pltpu.VMEM((2, 4, 144, 256), BF16),
+        pltpu.VMEM((4, 144, 256), F32),
+        pltpu.VMEM((2, 4, 144, 256), BF16),
+        pltpu.VMEM((16, 512), F32),
+        pltpu.VMEM((16, 512), F32),
+        pltpu.VMEM((2, 512, 512), BF16),
+        pltpu.VMEM((2, 16, SLAB, 512), BF16),
+        pltpu.VMEM((2, 16, HALF, 512), BF16),
+        pltpu.VMEM((2, 2, 4, HALF, 512), BF16),
+        pltpu.VMEM((2, 4, HALF, 512), BF16),
+        pltpu.VMEM((2, 3, HALF, 512), BF16),
+        pltpu.VMEM((2, HALF, 512), F32),
+        pltpu.VMEM((SLAB, 512), F32),
+        dma((11,)), dma((2, 4)), dma((2, 4)), dma((3,)), dma((2, 2, 4, 16)), dma((2, 2, 4, 16)), dma((2, 2)),
+    ]
+    return pl.pallas_call(
+        backward_kernel,
+        out_shape=[sds((2, 512, 512), BF16)]
+        + [sds((32, 512), F32)] * 4
+        + [sds((32, 2048), F32), sds((128, 512), F32), sds((8, 512), F32)],
+        in_specs=[vm, pl.BlockSpec(memory_space=pltpu.SMEM)] + [hbm] * len(saved),
+        out_specs=[vm] * 8,
+        scratch_shapes=scratch,
+        compiler_params=pltpu.CompilerParams(
+            collective_id=1, has_side_effects=True, vmem_limit_bytes=VMEM_LIMIT
+        ),
+        name="backward",
+    )(cotangent, lengths, *saved)
+
+
+def fast_local(inputs, cotangent, doc_lengths, feature_proj, *weights):
+    gain_rows = make_gain_rows(weights[6][0], weights[7][0])
+    outs = forward_call(inputs, doc_lengths, weights[:6], gain_rows, feature_proj)
+    gin, *grads = backward_call(cotangent, doc_lengths, outs[1:])
+    return (
+        (outs[0][None, :, None], gin[None, :, None])
+        + tuple(g[None] for g in grads[:6])
+        + (grads[6][0:1, 0:32], grads[6][1:2, 0:32])
+    )
+
 
 HIGH_PRECISION = lax.Precision.HIGHEST
 
@@ -360,4 +1311,6 @@
         P("section", ("dp", "seq")),
         P("section", ("dp", "seq")),
     )
-    return jax.shard_map(local, mesh=mesh, in_specs=in_specs, out_specs=out_specs, check_vma=False)
+    fits = mesh.shape["section"] == 2 and mesh.shape["dp"] == 4 and mesh.shape["seq"] == 4
+    body = fast_local if fits else local
+    return jax.shard_map(body, mesh=mesh, in_specs=in_specs, out_specs=out_specs, check_vma=False)

time: 1490 us -> 233 us (0.16)
  matrix products: 630 us -> 0 us
  waiting for transfers between devices: 357 us -> 0 us
  blocking collectives: 297 us -> 0 us
  Pallas kernels: 0 us -> 221 us
  local copies, waits for them, and re-layouts: 84.2 us -> 8.79 us
  other arithmetic: 61.8 us -> 2.02 us
  between operations: 24.3 us -> 0.71 us
  starting transfers between devices: 22.4 us -> 0 us
    dot_general x138 -> x0, matrix products: 630 us -> none  [the longest x12 159 us: attend(): jnp.einsum('thm,shm->hts', query_features, feats_k, precision=HIGH_PRECIS...]
    reduce_scatter x6 -> x0, waiting for transfers between devices: 292 us -> none  [local(): lax.psum_scatter(totals, ('dp', 'seq'), scatter_dimension=0, tiled=True)]
    pallas_call x0 -> x2, Pallas kernels: none -> 221 us  [the longest x1 117 us: backward_call(): pl.pallas_call(backward_kernel, out_shape=[sds((2, 512, 512), BF16)] + [s...]
    all_gather x10 -> x0, blocking collectives: 220 us -> none  [the longest x4 142 us: local(): lax.all_gather(as_sent(lowered), ('dp', 'seq'), axis=0, tiled=True)]
    unnamed x3 -> x0, blocking collectives: 76.7 us -> none
    all_gather x8 -> x0, waiting for transfers between devices: 65 us -> none  [the longest x2 65 us: local(): lax.all_gather(as_sent(lowered), ('dp', 'seq'), axis=0, tiled=True)]
    unnamed x670 -> x22, local copies, waits for them, and re-layouts: 44.7 us -> 7.24 us
    convert_element_type x35 -> x0, other arithmetic: 24.9 us -> none  [the longest x6 5.01 us: doc_masks(): same_doc = ((doc_ids[:, None] == doc_ids[None, :]) & (order_idx[None, :]...]
  transfers between devices with their start and end apart: 18 -> 0, of which waited for: 6 -> 0; matrix products, arithmetic and copies ran while one was open for 29% -> 0% of each run, Pallas kernels for 0% -> 0%
where the time goes in v1:
time: 233 us
  Pallas kernels  221 us (95%)
  local copies, waits for them, and re-layouts  8.79 us (4%)
    pallas_call x1, Pallas kernels, backward_call(): pl.pallas_call(backward_kernel, out_shape=[sds((2, 512, 512), BF16)] + [s...  117 us
    pallas_call x1, Pallas kernels, forward_call(): pl.pallas_call(forward_kernel, out_shape=[sds((2, 512, 512), BF16)] + sav...  104 us
    unnamed x22, local copies, waits for them, and re-layouts  7.24 us

profile of v1, /device:TPU:27, one launch (start us, length us, event | category | flops | bytes accessed | tf_op | source)
XLA Modules:
  0.0 232.8 jit_solution(10504414546974394645)
XLA Ops:
  0.6 0.7 convert_bitcast_fusion.1
  1.3 0.7 convert_bitcast_fusion
  2.0 0.1 pad.2.clone
  2.1 0.1 tile.27
  2.1 0.1 tile.24
  2.2 0.7 maximum_maximum_fusion.gains_in
  2.9 104.4 %forward.1 = (bf16[2,512,512]{2,1,0:T(8,128)(2,1)}, bf16[2,16,416,512]{3,2,1,0:T(8,128)(2,1)}, bf16[2,4,512,512]{3,2,1,0:T(8,128)(2,1)}, bf16[2,4,512,512]{3,2,1...) custom-call(bf16[2,1,512,512]{3,2,1,0:T(8,128)(2,1)} %inputs.1, ...), custom_call_target="tpu_custom_call" | custom-call | tf_op jit(solution)/shard_map/forward/pallas_call | solution.py:472
  107.3 117.0 %backward.1 = (bf16[2,512,512]{2,1,0:T(8,128)(2,1)}, f32[32,512]{1,0:T(8,128)}, f32[32,512]{1,0:T(8,128)}, f32[32,512]{1,0:T(8,128)}, f32[32,512]{1,0:T(8,128)},...) custom-call(bf16[2,1,512,512]{3,2,1,0:T(8,128)(2,1)} %cotangent.1, s32[2,1,4]{2,1,0:T(1,128)} %lengths.3, ...), custom_call_target="tpu_custom_call" | custom-call | tf_op jit(solution)/shard_map/backward/pallas_call | solution.py:931
  224.3 0.0 copy-start
  224.3 1.3 fusion
  225.6 0.0 copy-start.6
  225.6 0.0 copy-start.5
  225.6 0.0 copy-start.4
  225.6 0.0 copy-start.3
  225.6 0.0 copy-start.2
  225.6 2.3 copy.32
  227.9 0.0 copy-done
  227.9 0.0 copy-start.1
  227.9 1.0 copy.33
  228.9 0.0 copy-done.6
  228.9 0.6 copy.34
  229.5 0.0 copy-done.5
  229.5 0.6 copy.35
  230.2 0.0 copy-done.4
  230.2 0.6 copy.36
  230.8 0.0 copy-done.3
  230.8 0.6 copy.37
  231.4 0.0 copy-done.2
  231.4 0.7 copy.38
  232.1 0.0 copy-done.1
  232.1 0.7 copy.39
  (4 shorter events, 0.0 us)
Async XLA Ops:
  224.3 3.6 %copy-start = (bf16[2,512,512]{2,1,0:T(8,128)(2,1)S(1)}, bf16[2,512,512]{2,1,0:T(8,128)(2,1)}, u32[]{:S(2)}) copy-start(bf16[2,512,512]{2,1,0:T(8,128)(2,1)} %get-tuple-element.42) | copy-start | bytes 3145732
  225.6 3.3 %copy-start.6 = (f32[32,512]{1,0:T(8,128)S(1)}, f32[32,512]{1,0:T(8,128)}, u32[]{:S(2)}) copy-start(f32[32,512]{1,0:T(8,128)} %get-tuple-element.43) | copy-start | bytes 196612
  225.6 4.0 %copy-start.5 = (f32[32,512]{1,0:T(8,128)S(1)}, f32[32,512]{1,0:T(8,128)}, u32[]{:S(2)}) copy-start(f32[32,512]{1,0:T(8,128)} %get-tuple-element.44) | copy-start | bytes 196612
  225.6 4.6 %copy-start.4 = (f32[32,512]{1,0:T(8,128)S(1)}, f32[32,512]{1,0:T(8,128)}, u32[]{:S(2)}) copy-start(f32[32,512]{1,0:T(8,128)} %get-tuple-element.45) | copy-start | bytes 196612
  225.6 5.2 %copy-start.3 = (f32[32,512]{1,0:T(8,128)S(1)}, f32[32,512]{1,0:T(8,128)}, u32[]{:S(2)}) copy-start(f32[32,512]{1,0:T(8,128)} %get-tuple-element.46) | copy-start | bytes 196612
  225.6 5.8 %copy-start.2 = (f32[32,2048]{1,0:T(8,128)S(1)}, f32[32,2048]{1,0:T(8,128)}, u32[]{:S(2)}) copy-start(f32[32,2048]{1,0:T(8,128)} %get-tuple-element.47) | copy-start | bytes 786436
  227.9 4.2 %copy-start.1 = (f32[128,512]{1,0:T(8,128)S(1)}, f32[128,512]{1,0:T(8,128)}, u32[]{:S(2)}) copy-start(f32[128,512]{1,0:T(8,128)} %get-tuple-element.48) | copy-start | bytes 786436

commit v2 on v1

--- a/solution.py
+++ b/solution.py
@@ -57,12 +57,12 @@
         out = [self.sibling(), self.at(self.xn, self.z), self.at(self.yn, self.z)]
         return out + [self.at(self.d, lax.rem(self.z + k, 4)) for k in (1, 2, 3)]
 
-    def barrier(self):
-        bar = pltpu.get_barrier_semaphore()
-        peers = self.peers()
-        for dev in peers:
-            pl.semaphore_signal(bar, inc=1, device_id=dev, device_id_type=MESH)
-        pl.semaphore_wait(bar, len(peers))
+    def greet(self):
+        for dev in self.peers():
+            pl.semaphore_signal(pltpu.get_barrier_semaphore(), inc=1, device_id=dev, device_id_type=MESH)
+
+    def meet(self):
+        pl.semaphore_wait(pltpu.get_barrier_semaphore(), len(self.peers()))
 
 
 def weight(G, l, row, n=32):
@@ -194,6 +194,7 @@
 ):
     pc = Place()
     c, z = pc.c, pc.z
+    pc.greet()
     G[c, pc.me, 0:ROW_Q, :] = gains_in[...]
     for ref, row in ((wq_in, ROW_Q), (wk_in, ROW_K), (wv_in, ROW_V), (wo_in, ROW_O)):
         G[c, pc.me, row : row + 32, :] = ref[0].astype(BF16)
@@ -204,7 +205,7 @@
     hi = proj[0].astype(BF16)
     px[c, 0] = hi
     px[c, 1] = (proj[0] - hi.astype(F32)).astype(BF16)
-    pc.barrier()
+    pc.meet()
     halves = {}
     for por, (base, n) in enumerate(PORTIONS):
         for half, at in ((0, pc.o), (1, c)):
@@ -251,6 +252,8 @@
                 pk[l, p, 128 + 64 * h : 192 + 64 * h, to] = jnp.full((64, 256), -0.5, BF16)
                 pk[l, p, 256 + 64 * h : 320 + 64 * h, to] = px[l, 0, 2 * p + h]
                 pk[l, p, 384 + 64 * h : 448 + 64 * h, to] = px[l, 1, 2 * p + h]
+    keep = pltpu.make_async_copy(pk.at[:, :, 0:256, :], pb_out, osem)
+    keep.start()
     vext[:, :, :, 128:] = jnp.ones((2, 4, 512, 128), BF16)
 
     @pl.when(z == 0)
@@ -275,6 +278,26 @@
     def chain(l, p):
         return remote(sbuf.at[l, p], sin.at[l, p], csend.at[l, p], crecv.at[l, p], below)
 
+    saved = (
+        (G, G_out), (fq, fq_out), (fk, fk_out), (vext, v_out), (att, att_out), (rden, rden_out),
+        (branch, branch_out), (wqk, w_out), (xin, x_out), (sin, sin_out),
+    )
+
+    def save(l, *refs):
+        for i, (src, dst) in enumerate(saved):
+            if any(src is ref for ref in refs):
+                pltpu.make_async_copy(src.at[l], dst.at[l], wsem.at[l, i]).start()
+
+    def give_own(l):
+        return pltpu.make_async_copy(ybuf.at[l], act.at[c], asem.at[0])
+
+    def give_far(l):
+        return remote(ybuf.at[l], act.at[c], asem.at[1], asem.at[2], pc.sibling())
+
+    def give(l):
+        pl.when(c == l)(lambda: give_own(l).start())
+        pl.when(c != l)(lambda: give_far(l).start())
+
     def layer(l, during):
         gains[...] = jnp.sum(G[l, :, 0:16, :].astype(F32), axis=0)
 
@@ -289,6 +312,11 @@
         scale = 64 ** (-0.25)
         kbuf[...] = dot(hbuf[...], weight(G, l, ROW_K)) * scale
         qbuf[...] = dot(hbuf[...], weight(G, l, ROW_V))
+
+        def pass_on(p):
+            chain(l, p).wait_recv()
+            sbuf[l, p] = (tail[p] + sin[l, p].astype(F32)).astype(BF16)
+            chain(l, p).start()
 
         def key_pair(p, _):
             if "key" in during:
@@ -309,9 +337,14 @@
                 sbuf[l, p] = t.astype(BF16)
                 chain(l, p).start()
 
+            @pl.when((z == 1) & (p >= 2))
+            def _():
+                pass_on(p - 2)
+
             return 0
 
         lax.fori_loop(0, 4, key_pair, 0)
+        save(l, fk, vext, xin)
         qbuf[...] = dot(hbuf[...], weight(G, l, ROW_Q)) * scale
 
         def query_pair(p, _):
@@ -321,23 +354,32 @@
             w = qbuf[:, at]
             wqk[l, 0, p] = w.astype(BF16)
             fq[l, p] = lift_pair(w, pk[l, p])
+
+            @pl.when((z == 1) & (p < 2))
+            def _():
+                pass_on(p + 2)
+
+            @pl.when((z == 2) & (p >= 1))
+            def _():
+                pass_on(p - 1)
+
             return 0
 
         lax.fori_loop(0, 4, query_pair, 0)
+        save(l, fq, wqk)
 
         def attend_pair(p, _):
             if "attend" in during:
                 during["attend"](p)
             at = pl.ds(pl.multiple_of(p * 128, 128), 128)
 
-            @pl.when(z > 0)
+            @pl.when((z == 2) & (p == 0))
+            def _():
+                pass_on(3)
+
+            @pl.when(z == 3)
             def _():
                 chain(l, p).wait_recv()
-
-            @pl.when((z > 0) & (z < 3))
-            def _():
-                sbuf[l, p] = (tail[p] + sin[l, p].astype(F32)).astype(BF16)
-                chain(l, p).start()
 
             for t in (0, 1):
                 n = 256 * (t + 1)
@@ -360,6 +402,7 @@
             return 0
 
         lax.fori_loop(0, 4, attend_pair, 0)
+        save(l, att, rden, sin)
 
         if "branch" in during:
             during["branch"]()
@@ -372,7 +415,9 @@
             acc[at, :] = b
             return 0
 
+        save(l, G)
         lax.fori_loop(0, 2, branch_tile, 0)
+        save(l, branch)
 
         def ffn_tile(j, _):
             if "ffn" in during:
@@ -390,13 +435,7 @@
         y = acc[...].astype(BF16)
         ybuf[l] = y
         xbuf[...] = y.astype(F32)
-        for i, (src, dst) in enumerate(saved):
-            pltpu.make_async_copy(src.at[l], dst.at[l], wsem.at[l, i]).start()
-
-    saved = (
-        (G, G_out), (fq, fq_out), (fk, fk_out), (vext, v_out), (att, att_out), (rden, rden_out),
-        (branch, branch_out), (wqk, w_out), (xin, x_out), (sin, sin_out),
-    )
+        give(l)
 
     def before_branch(l):
         if l == 0:
@@ -408,14 +447,8 @@
     four(moves[1, 0].far)
     moves[1, 0].finish()
     layer(1, {"query": moves[1, 1].far, "branch": lambda: before_branch(1)})
-    keep = pltpu.make_async_copy(pk.at[:, :, 0:256, :], pb_out, osem)
-    keep.start()
-    own_act = pltpu.make_async_copy(ybuf.at[c], act.at[c], asem.at[0])
-    own_act.start()
-    far_act = remote(ybuf.at[pc.o], act.at[c], asem.at[1], asem.at[2], pc.sibling())
-    far_act.start()
-    own_act.wait()
-    far_act.wait()
+    give_own(0).wait()
+    give_far(0).wait()
     keep.wait()
     for l in (0, 1):
         for i, (src, dst) in enumerate(saved):
@@ -507,8 +540,8 @@
     return rstd * (dy - m1 - y * m2)
 
 
-HALF = SLAB // 2
-SUM_PORTIONS = ((ROW_UP, 128), (0, 80))
+HALF = (SLAB - ROW_Q) // 2
+SUM_PORTIONS = ((ROW_O, 144), (ROW_Q, 48))
 
 
 class Sums:
@@ -606,27 +639,41 @@
 
 
 def backward_kernel(
-    cotangent, lengths, G_in, fq_in, fk_in, v_in, att_in, rden_in, branch_in, w_in, x_in, sin_in, pb_in,
+    cotangent, lengths, wq_in, wk_in, wv_in, wup_in, G_in, fq_in, fk_in, v_in, att_in, rden_in, branch_in, w_in, x_in, sin_in, pb_in,
     gin, gq_out, gk_out, gv_out, go_out, gup_out, gdown_out, gg_out,
     G, fq, fk, vext, att, rden, branch, wqk, xin, sin, pb,
-    mask, mask_t, gbuf, gbr, hbuf, hT, gb, dh, gq, gk, gv, le, rin, rtail, rbuf, gains, gsum, xout, slabs,
+    mask, mask_t, gbuf, gbr, hbuf, hT, gb, dh, gq, gk, gv, le, rin, rtail, rbuf, gains, xout, slabs,
     sb, r1, r2, r3, keep, total,
     lsem, csend, crecv, asem, ssem, rsem, fsem,
 ):
     pc = Place()
     c, z = pc.c, pc.z
-    loads = (
-        (G_in, G), (fq_in, fq), (fk_in, fk), (v_in, vext), (att_in, att), (rden_in, rden), (branch_in, branch),
-        (w_in, wqk), (x_in, xin), (sin_in, sin), (pb_in, pb),
-    )
-
-    def load(l, i):
-        src, dst = loads[i]
-        return pltpu.make_async_copy(src.at[l], dst, lsem.at[i])
-
-    pc.barrier()
-    for i in range(len(loads)):
-        load(1, i).start()
+    top, attn, ffn = pl.ds(0, 16), pl.ds(ROW_Q, ROW_UP - ROW_Q), pl.ds(ROW_UP, SLAB - ROW_UP)
+    loads = {
+        "branch": (lambda l: branch_in.at[l], branch), "top": (lambda l: G_in.at[l, :, top], G.at[:, top]),
+        "ffn": (lambda l: G_in.at[l, :, ffn], G.at[:, ffn]), "att": (lambda l: att_in.at[l], att),
+        "attn": (lambda l: G_in.at[l, :, attn], G.at[:, attn]), "rden": (lambda l: rden_in.at[l], rden),
+        "fq": (lambda l: fq_in.at[l], fq), "sin": (lambda l: sin_in.at[l], sin), "fk": (lambda l: fk_in.at[l], fk),
+        "vext": (lambda l: v_in.at[l], vext), "pb": (lambda l: pb_in.at[l], pb), "wqk": (lambda l: w_in.at[l], wqk),
+        "xin": (lambda l: x_in.at[l], xin),
+    }
+
+    def load(l, name):
+        src, dst = loads[name]
+        return pltpu.make_async_copy(src(l), dst, lsem.at[list(loads).index(name)])
+
+    def needs(l, *names):
+        for name in names:
+            load(l, name).wait()
+
+    def done(l, *names):
+        if l == 1:
+            for name in names:
+                load(0, name).start()
+
+    pc.greet()
+    for name in loads:
+        load(1, name).start()
 
     first_row = z * 512
     rows = lax.broadcasted_iota(jnp.int32, (512, 512), 0)
@@ -650,6 +697,7 @@
         rin[...] = jnp.zeros_like(rin)
 
     gbuf[...] = cotangent[c, 0].astype(F32)
+    pc.meet()
     above = (c, pc.d, jnp.maximum(z - 1, 0))
     row_low = lax.broadcasted_iota(jnp.int32, (144, 256), 0)
     tail_is_first = (row_low < 64) | ((row_low >= 128) & (row_low < 136))
@@ -672,10 +720,8 @@
             if name in during:
                 during[name](*args)
 
-        for i in range(len(loads)):
-            load(l, i).wait()
+        needs(l, "branch", "top")
         gains[...] = jnp.sum(G[:, 0:16, :].astype(F32), axis=0)
-        gsum[...] = jnp.zeros_like(gsum)
 
         def norm_tile(i, _):
             at = pl.ds(pl.multiple_of(i * 128, 128), 128)
@@ -703,16 +749,16 @@
             dh[...] += dot_nt(g, up)
             return 0
 
+        needs(l, "ffn")
         lax.fori_loop(0, 4, ffn_tile, 0)
-
-        sums[l, 0].begin()
+        done(l, "top", "ffn")
+        needs(l, "att")
 
         def branch_tile(i, _):
             at_point("branch", i)
             at = pl.ds(pl.multiple_of(i * 128, 128), 128)
             y, rstd = norm(branch[at, :])
             d = dh[at, :]
-            gsum[1:2, :] += jnp.sum(d * y, axis=0, keepdims=True)
             g = gbuf[at, :] + norm_back(y, rstd, d * gains[1:2, :])
             gbr[at, :] = g
             gb[at, :] = g.astype(BF16)
@@ -720,8 +766,17 @@
             return 0
 
         lax.fori_loop(0, 4, branch_tile, 0)
+        done(l, "branch")
         put(l, ROW_O, 32, dot_tn(hbuf[...], gb[...]))
+        sums[l, 0].begin()
+        at_point("middle")
+        needs(l, "attn", "rden", "fq")
         dh[...] = dot_nt(gb[...], G[:, ROW_O : ROW_O + 32, :].reshape(512, 512))
+
+        def pass_on(p):
+            chain(l, p).wait_recv()
+            rbuf[l, p] = (rtail[p] + rin[l, p].astype(F32)).astype(BF16)
+            chain(l, p).start()
 
         def tail_pair(p, _):
             at_point("tail", p)
@@ -744,52 +799,65 @@
                 rbuf[l, p] = tl.astype(BF16)
                 chain(l, p).start()
 
+            @pl.when((z == 2) & (p >= 3))
+            def _():
+                pass_on(p - 3)
+
             return 0
 
         lax.fori_loop(0, 4, tail_pair, 0)
+        done(l, "att", "rden")
+        needs(l, "sin", "fk", "vext", "pb", "wqk")
 
         def attend_pair(p, _):
             at_point("attend", p)
             at = pl.ds(pl.multiple_of(p * 128, 128), 128)
 
-            @pl.when(z < 3)
+            @pl.when((z == 2) & (p < 3))
             def _():
-                chain(l, p).wait_recv()
-
-            @pl.when((z > 0) & (z < 3))
-            def _():
-                rbuf[l, p] = (rtail[p] + rin[l, p].astype(F32)).astype(BF16)
-                chain(l, p).start()
+                pass_on(p + 1)
 
             ve = vext[p]
             lep = le[p]
             dq, dk, dv = [], [], []
             for h in (0, 1):
+                if h == 1:
+                    @pl.when(z == 1)
+                    def _():
+                        pass_on(p)
+
                 fl = slice(256 * h, 256 * h + 256)
                 keep = lane_low((512, 256)) if h == 0 else jnp.logical_not(lane_low((512, 256)))
                 leh = jnp.where(keep, lep, jnp.zeros((), BF16))
                 fqh, fkh = fq[p, :, fl], fk[p, :, fl]
                 zrow = sin[p, 128:144, :].astype(F32)[8 * h : 8 * h + 1, :]
                 st = jnp.concatenate([sin[p, 0:128, :], jnp.broadcast_to(zrow, (128, 256)).astype(BF16)], axis=0)
-                rrow = rin[l, p, 128:144, :].astype(F32)[8 * h : 8 * h + 1, :] * (1.0 / 128.0)
-                rows_h = lax.broadcasted_iota(jnp.int32, (128, 256), 0) // 64 == h
-                rt = jnp.where(rows_h, rin[l, p, 0:128, :], jnp.zeros((), BF16))
-                rte = jnp.concatenate([rt, jnp.broadcast_to(rrow, (128, 256)).astype(BF16)], axis=0)
                 dqh = head_col * dot(leh, st)
                 da0 = dot_nt(leh[0:256], ve[0:256]).astype(BF16) * mask[0:256, 0:256]
                 da1 = dot_nt(leh[256:512], ve).astype(BF16) * mask[256:512, :]
                 dqh = dqh + jnp.concatenate([dot(da0, fkh[0:256]), dot(da1, fkh)], axis=0)
                 at0 = dot_nt(fkh[0:256], fqh).astype(BF16) * mask_t[0:256, :]
                 at1 = dot_nt(fkh[256:512], fqh[256:512]).astype(BF16) * mask_t[256:512, 256:512]
-                dvh = tail_col * dot_nt(fkh, rin[l, p, 0:128, :])
-                dvh = dvh + jnp.concatenate([dot(at0, lep[:, 0:128]), dot(at1, lep[256:512, 0:128])], axis=0)
+                dvh = jnp.concatenate([dot(at0, lep[:, 0:128]), dot(at1, lep[256:512, 0:128])], axis=0)
                 dt0 = dot_nt(ve[0:256], leh).astype(BF16) * mask_t[0:256, :]
                 dt1 = dot_nt(ve[256:512], leh[256:512]).astype(BF16) * mask_t[256:512, 256:512]
-                dkh = tail_col * dot(ve, rte)
-                dkh = dkh + jnp.concatenate([dot(dt0, fqh), dot(dt1, fqh[256:512])], axis=0)
+                dkh = jnp.concatenate([dot(dt0, fqh), dot(dt1, fqh[256:512])], axis=0)
                 dq.append((dqh * fqh.astype(F32)).astype(BF16))
-                dk.append((dkh * fkh.astype(F32)).astype(BF16))
+                dk.append(dkh)
                 dv.append(dvh)
+
+            @pl.when(z == 0)
+            def _():
+                chain(l, p).wait_recv()
+
+            for h in (0, 1):
+                fkh = fk[p, :, 256 * h : 256 * h + 256]
+                rrow = rin[l, p, 128:144, :].astype(F32)[8 * h : 8 * h + 1, :] * (1.0 / 128.0)
+                rows_h = lax.broadcasted_iota(jnp.int32, (128, 256), 0) // 64 == h
+                rt = jnp.where(rows_h, rin[l, p, 0:128, :], jnp.zeros((), BF16))
+                rte = jnp.concatenate([rt, jnp.broadcast_to(rrow, (128, 256)).astype(BF16)], axis=0)
+                dv[h] = dv[h] + tail_col * dot_nt(fkh, rin[l, p, 0:128, :])
+                dk[h] = ((dk[h] + tail_col * dot(ve, rte)) * fkh.astype(F32)).astype(BF16)
             gv[:, at] = jnp.where(low, dv[0], dv[1]).astype(BF16)
             for k, e, out in ((0, dq, gq), (1, dk, gk)):
                 gw = dot_nt(jnp.concatenate(e, axis=1), pb[p])
@@ -798,6 +866,8 @@
             return 0
 
         lax.fori_loop(0, 4, attend_pair, 0)
+        done(l, "fq", "sin", "fk", "vext", "pb", "wqk")
+        needs(l, "xin")
 
         def norm_tile2(i, _):
             at_point("norm", i)
@@ -809,42 +879,42 @@
         hT[...] = hbuf[...].T
         for row, g in ((ROW_Q, gq), (ROW_K, gk), (ROW_V, gv)):
             put(l, row, 32, dot(hT[...], g[...]))
+        sums[l, 1].begin()
         dh[...] = dot_nt(gq[...], G[:, ROW_Q : ROW_Q + 32, :].reshape(512, 512))
         dh[...] += dot_nt(gk[...], G[:, ROW_K : ROW_K + 32, :].reshape(512, 512))
         dh[...] += dot_nt(gv[...], G[:, ROW_V : ROW_V + 32, :].reshape(512, 512))
+
+        done(l, "attn")
+        at_point("late")
 
         def out_tile(i, _):
             at_point("out", i)
             at = pl.ds(pl.multiple_of(i * 128, 128), 128)
             y, rstd = norm(xin[at, :].astype(F32))
             d = dh[at, :]
-            gsum[0:1, :] += jnp.sum(d * y, axis=0, keepdims=True)
             g = (gbr[at, :] + norm_back(y, rstd, d * gains[0:1, :])).astype(BF16)
             xout[l, at, :] = g
             gbuf[at, :] = g.astype(F32)
             return 0
 
         lax.fori_loop(0, 4, out_tile, 0)
-        slabs[l, :, 0:16, :] = jnp.broadcast_to(gsum[...].astype(BF16)[None], (16, 16, 512))
-        slabs[l, :, 16:32, :] = jnp.zeros((16, 16, 512), BF16)
-
-        sums[l, 1].begin()
-        if l == 1:
-            for i in range(len(loads)):
-                load(0, i).start()
-
+        done(l, "xin")
 
     def four(step, *args):
         for i in range(4):
             step(*args, i)
 
+    def along_z(m):
+        for k in (1, 2, 3, 0):
+            m.stage3(k)
+
     layer(1, {"tail": lambda p: sums[1, 0].stage1(0, p), "attend": lambda p: sums[1, 0].stage1(1, p),
               "norm": sums[1, 0].stage2})
-    for k in (1, 2, 3, 0):
-        sums[1, 0].stage3(k)
+    along_z(sums[1, 0])
     layer(0, {"ffn": lambda p: (sums[1, 1].stage1(0, p), sums[1, 1].stage1(1, p)), "branch": sums[1, 1].stage2,
+              "middle": lambda: along_z(sums[1, 1]),
               "tail": lambda p: sums[0, 0].stage1(0, p), "attend": lambda p: sums[0, 0].stage1(1, p),
-              "norm": sums[0, 0].stage2})
+              "norm": sums[0, 0].stage2, "out": lambda i: (sums[0, 1].stage1(0, i), sums[0, 1].stage1(1, i))})
     own_act = pltpu.make_async_copy(xout.at[c], gin.at[c], asem.at[0])
     own_act.start()
     far_act = remote(xout.at[pc.o], gin.at[c], asem.at[1], asem.at[2], pc.sibling())
@@ -852,15 +922,9 @@
     own_act.wait()
     far_act.wait()
 
-    four(sums[0, 1].stage1, 0)
-    four(sums[0, 1].stage1, 1)
-    for k in (1, 2, 3, 0):
-        sums[1, 1].stage3(k)
-    for k in (1, 2, 3, 0):
-        sums[0, 0].stage3(k)
+    along_z(sums[0, 0])
     four(sums[0, 1].stage2)
-    for k in (1, 2, 3, 0):
-        sums[0, 1].stage3(k)
+    along_z(sums[0, 1])
     for m in sums.values():
         m.arrive()
     for por in (0, 1):
@@ -882,7 +946,15 @@
     for j in range(4):
         gup_out[:, 512 * j : 512 * j + 512] = total[ROW_UP + 32 * j : ROW_UP + 32 * j + 32, :]
     gdown_out[...] = total[ROW_DOWN:SLAB, :]
-    gg_out[...] = pltpu.roll(total[0:8, :], lax.rem(512 - 32 * pc.me, 512), 1)
+    ga = jnp.zeros((32, 512), F32)
+    for ref, row in ((wq_in, ROW_Q), (wk_in, ROW_K), (wv_in, ROW_V)):
+        ga = ga + ref[0].astype(BF16).astype(F32) * total[row : row + 32, :]
+    gf = jnp.zeros((32, 512), F32)
+    for j in range(4):
+        up = wup_in[0, :, 512 * j : 512 * j + 512].astype(BF16).astype(F32)
+        gf = gf + up * total[ROW_UP + 32 * j : ROW_UP + 32 * j + 32, :]
+    gg_out[0] = jnp.broadcast_to(jnp.sum(ga, axis=1, keepdims=True), (32, 128))
+    gg_out[1] = jnp.broadcast_to(jnp.sum(gf, axis=1, keepdims=True), (32, 128))
     for m in sums.values():
         m.drain()
 
@@ -893,7 +965,7 @@
                 chain(l, p).wait_send()
 
 
-def backward_call(cotangent, lengths, saved):
+def backward_call(cotangent, lengths, weights, saved):
     sds = jax.ShapeDtypeStruct
     dma = pltpu.SemaphoreType.DMA
     vm = pl.BlockSpec(memory_space=pltpu.VMEM)
@@ -917,7 +989,6 @@
         pltpu.VMEM((4, 144, 256), F32),
         pltpu.VMEM((2, 4, 144, 256), BF16),
         pltpu.VMEM((16, 512), F32),
-        pltpu.VMEM((16, 512), F32),
         pltpu.VMEM((2, 512, 512), BF16),
         pltpu.VMEM((2, 16, SLAB, 512), BF16),
         pltpu.VMEM((2, 16, HALF, 512), BF16),
@@ -926,31 +997,36 @@
         pltpu.VMEM((2, 3, HALF, 512), BF16),
         pltpu.VMEM((2, HALF, 512), F32),
         pltpu.VMEM((SLAB, 512), F32),
-        dma((11,)), dma((2, 4)), dma((2, 4)), dma((3,)), dma((2, 2, 4, 16)), dma((2, 2, 4, 16)), dma((2, 2)),
+        dma((13,)), dma((2, 4)), dma((2, 4)), dma((3,)), dma((2, 2, 4, 16)), dma((2, 2, 4, 16)), dma((2, 2)),
     ]
     return pl.pallas_call(
         backward_kernel,
         out_shape=[sds((2, 512, 512), BF16)]
         + [sds((32, 512), F32)] * 4
-        + [sds((32, 2048), F32), sds((128, 512), F32), sds((8, 512), F32)],
-        in_specs=[vm, pl.BlockSpec(memory_space=pltpu.SMEM)] + [hbm] * len(saved),
+        + [sds((32, 2048), F32), sds((128, 512), F32), sds((2, 32, 128), F32)],
+        in_specs=[vm, pl.BlockSpec(memory_space=pltpu.SMEM)] + [vm] * 4 + [hbm] * len(saved),
         out_specs=[vm] * 8,
         scratch_shapes=scratch,
         compiler_params=pltpu.CompilerParams(
             collective_id=1, has_side_effects=True, vmem_limit_bytes=VMEM_LIMIT
         ),
         name="backward",
-    )(cotangent, lengths, *saved)
+    )(cotangent, lengths, *weights, *saved)
 
 
 def fast_local(inputs, cotangent, doc_lengths, feature_proj, *weights):
     gain_rows = make_gain_rows(weights[6][0], weights[7][0])
     outs = forward_call(inputs, doc_lengths, weights[:6], gain_rows, feature_proj)
-    gin, *grads = backward_call(cotangent, doc_lengths, outs[1:])
+    w_query, w_key, w_value, _, w_up = weights[:5]
+    gin, *grads = backward_call(cotangent, doc_lengths, (w_query, w_key, w_value, w_up), outs[1:])
+
+    def by_gain(sums, gain):
+        return sums[None, :, 0] / gain.astype(BF16).astype(F32)
+
     return (
         (outs[0][None, :, None], gin[None, :, None])
         + tuple(g[None] for g in grads[:6])
-        + (grads[6][0:1, 0:32], grads[6][1:2, 0:32])
+        + (by_gain(grads[6][0], weights[6]), by_gain(grads[6][1], weights[7]))
     )
 
 

time: 233 us -> 214 us (0.918)
  Pallas kernels: 221 us -> 201 us
    pallas_call x1, Pallas kernels: 117 us -> 103 us  [backward_call(): pl.pallas_call(backward_kernel, out_shape=[sds((2, 512, 512), BF16)] + [s...]
    pallas_call x1, Pallas kernels: 104 us -> 97.7 us  [forward_call(): pl.pallas_call(forward_kernel, out_shape=[sds((2, 512, 512), BF16)] + sav...]
    unnamed x22 -> x26, local copies, waits for them, and re-layouts: 7.24 us -> 7.25 us
where the time goes in v2:
time: 214 us
  Pallas kernels  201 us (94%)
  local copies, waits for them, and re-layouts  8.56 us (4%)
  other arithmetic  3.06 us (1%)
    pallas_call x1, Pallas kernels, backward_call(): pl.pallas_call(backward_kernel, out_shape=[sds((2, 512, 512), BF16)] + [s...  103 us
    pallas_call x1, Pallas kernels, forward_call(): pl.pallas_call(forward_kernel, out_shape=[sds((2, 512, 512), BF16)] + sav...  97.7 us
    unnamed x26, local copies, waits for them, and re-layouts  7.25 us

profile of v2, /device:TPU:27, one launch (start us, length us, event | category | flops | bytes accessed | tf_op | source)
XLA Modules:
  0.0 213.5 jit_solution(15322942055802899313)
XLA Ops:
  0.6 0.7 convert_bitcast_fusion.1
  1.3 0.7 convert_bitcast_fusion
  2.0 0.1 pad.2.clone
  2.1 0.1 tile.27
  2.1 0.1 tile.24
  2.2 0.7 maximum_maximum_fusion.gains_in
  2.9 97.7 %forward.1 = (bf16[2,512,512]{2,1,0:T(8,128)(2,1)}, bf16[2,16,416,512]{3,2,1,0:T(8,128)(2,1)}, bf16[2,4,512,512]{3,2,1,0:T(8,128)(2,1)}, bf16[2,4,512,512]{3,2,1...) custom-call(bf16[2,1,512,512]{3,2,1,0:T(8,128)(2,1)} %inputs.1, ...), custom_call_target="tpu_custom_call" | custom-call | tf_op jit(solution)/shard_map/forward/pallas_call | solution.py:505
  100.7 0.0 copy-start.7
  100.7 0.0 copy-start.8
  100.7 103.5 %backward.1 = (bf16[2,512,512]{2,1,0:T(8,128)(2,1)}, f32[32,512]{1,0:T(8,128)}, f32[32,512]{1,0:T(8,128)}, f32[32,512]{1,0:T(8,128)}, f32[32,512]{1,0:T(8,128)},...) custom-call(bf16[2,1,512,512]{3,2,1,0:T(8,128)(2,1)} %cotangent.1, s32[2,1,4]{2,1,0:T(1,128)} %lengths.3, ...), custom_call_target="tpu_custom_call" | custom-call | tf_op jit(solution)/shard_map/backward/pallas_call | solution.py:1002
  204.2 0.0 copy-start
  204.2 0.8 slice_bitcast_fusion
  205.0 0.1 slice_reduce_fusion
  205.1 0.0 copy-done.7
  205.1 0.5 bitcast_divide_fusion
  205.6 0.1 slice_reduce_fusion.1
  205.8 0.0 copy-done.8
  205.8 0.5 bitcast_divide_fusion.1
  206.3 0.0 copy-start.2
  206.3 2.3 %copy.34 = bf16[1,2,1,512,512]{4,3,2,1,0:T(8,128)(2,1)} copy(bf16[1,2,1,512,512]{4,3,2,1,0:T(8,128)(2,1)} %bitcast.24) | data formatting | bytes 2097152
  208.6 0.0 copy-done
  208.6 1.0 copy.35
  209.6 0.0 copy-done.6
  209.6 0.6 copy.36
  210.2 0.0 copy-done.5
  210.2 0.6 copy.37
  210.9 0.0 copy-done.4
  210.9 0.6 copy.38
  211.5 0.6 copy.39
  212.1 0.0 copy-done.2
  212.1 0.7 copy.40
  212.8 0.7 copy.41
  (11 shorter events, 0.0 us)
Async XLA Ops:
  100.7 104.4 %copy-start.7 = (f32[1,32]{1,0:T(1,128)S(1)}, f32[1,32]{1,0:T(1,128)}, u32[]{:S(2)}) copy-start(f32[1,32]{1,0:T(1,128)} %param.23) | copy-start | bytes 388
  100.7 105.1 %copy-start.8 = (f32[1,32]{1,0:T(1,128)S(1)}, f32[1,32]{1,0:T(1,128)}, u32[]{:S(2)}) copy-start(f32[1,32]{1,0:T(1,128)} %param.22) | copy-start | bytes 388
  204.2 4.5 %copy-start = (bf16[2,512,512]{2,1,0:T(8,128)(2,1)S(1)}, bf16[2,512,512]{2,1,0:T(8,128)(2,1)}, u32[]{:S(2)}) copy-start(bf16[2,512,512]{2,1,0:T(8,128)(2,1)} %get-tuple-element.42) | copy-start | bytes 3145732
  206.3 3.3 %copy-start.6 = (f32[32,512]{1,0:T(8,128)S(1)}, f32[32,512]{1,0:T(8,128)}, u32[]{:S(2)}) copy-start(f32[32,512]{1,0:T(8,128)} %get-tuple-element.43) | copy-start | bytes 196612
  206.3 3.9 %copy-start.5 = (f32[32,512]{1,0:T(8,128)S(1)}, f32[32,512]{1,0:T(8,128)}, u32[]{:S(2)}) copy-start(f32[32,512]{1,0:T(8,128)} %get-tuple-element.44) | copy-start | bytes 196612
  206.3 4.6 %copy-start.4 = (f32[32,512]{1,0:T(8,128)S(1)}, f32[32,512]{1,0:T(8,128)}, u32[]{:S(2)}) copy-start(f32[32,512]{1,0:T(8,128)} %get-tuple-element.45) | copy-start | bytes 196612
  206.3 5.2 %copy-start.3 = (f32[32,512]{1,0:T(8,128)S(1)}, f32[32,512]{1,0:T(8,128)}, u32[]{:S(2)}) copy-start(f32[32,512]{1,0:T(8,128)} %get-tuple-element.46) | copy-start | bytes 196612
  206.3 5.8 %copy-start.2 = (f32[32,2048]{1,0:T(8,128)S(1)}, f32[32,2048]{1,0:T(8,128)}, u32[]{:S(2)}) copy-start(f32[32,2048]{1,0:T(8,128)} %get-tuple-element.47) | copy-start | bytes 786436
  208.6 4.2 %copy-start.1 = (f32[128,512]{1,0:T(8,128)S(1)}, f32[128,512]{1,0:T(8,128)}, u32[]{:S(2)}) copy-start(f32[128,512]{1,0:T(8,128)} %get-tuple-element.48) | copy-start | bytes 786436

commit v3 on v2

--- a/solution.py
+++ b/solution.py
@@ -186,7 +186,7 @@
 
 
 def forward_kernel(
-    inputs, lengths, wq_in, wk_in, wv_in, wo_in, wup_in, wdown_in, gains_in, proj,
+    inputs, lengths, wq_in, wk_in, wv_in, wo_in, wup_in, wdown_in, ga_in, gf_in, proj,
     act, G_out, fq_out, fk_out, v_out, att_out, rden_out, branch_out, w_out, x_out, sin_out, pb_out,
     G, px, pk, mask, xbuf, hbuf, qbuf, kbuf, fq, fk, vext, att, rden, branch, wqk, xin, sin, tail, sbuf,
     gains, ybuf, hf, acc,
@@ -195,7 +195,12 @@
     pc = Place()
     c, z = pc.c, pc.z
     pc.greet()
-    G[c, pc.me, 0:ROW_Q, :] = gains_in[...]
+    gains[...] = jnp.zeros_like(gains)
+    gains[0:1, 0:32] = ga_in[...]
+    gains[1:2, 0:32] = gf_in[...]
+    placed = pltpu.roll(gains[0:8, :], 32 * pc.me, 1)
+    G[c, pc.me, 0:16, :] = jnp.concatenate([placed, jnp.zeros((8, 512), F32)], axis=0).astype(BF16)
+    G[c, pc.me, 16:ROW_Q, :] = jnp.zeros((ROW_Q - 16, 512), BF16)
     for ref, row in ((wq_in, ROW_Q), (wk_in, ROW_K), (wv_in, ROW_V), (wo_in, ROW_O)):
         G[c, pc.me, row : row + 32, :] = ref[0].astype(BF16)
     for j in range(4):
@@ -464,7 +469,7 @@
         move.drain()
 
 
-def forward_call(inputs, lengths, weights, gain_rows, proj):
+def forward_call(inputs, lengths, weights, proj):
     sds = jax.ShapeDtypeStruct
     dma = pltpu.SemaphoreType.DMA
     vm = pl.BlockSpec(memory_space=pltpu.VMEM)
@@ -505,25 +510,14 @@
     return pl.pallas_call(
         forward_kernel,
         out_shape=[sds((2, 512, 512), BF16)] + saved,
-        in_specs=[vm, pl.BlockSpec(memory_space=pltpu.SMEM)] + [vm] * 8,
+        in_specs=[vm, pl.BlockSpec(memory_space=pltpu.SMEM)] + [vm] * 9,
         out_specs=[vm] + [hbm] * len(saved),
         scratch_shapes=scratch,
         compiler_params=pltpu.CompilerParams(
             collective_id=0, has_side_effects=True, vmem_limit_bytes=VMEM_LIMIT
         ),
         name="forward",
-    )(inputs, lengths, *weights, gain_rows, proj)
-
-
-def make_gain_rows(gain_attn, gain_ffn):
-    g = lax.axis_index("dp") * 4 + lax.axis_index("seq")
-    lane = lax.broadcasted_iota(jnp.int32, (1, 512), 1)
-    mine = lane // 32 == g
-
-    def gain_row(gain):
-        return jnp.where(mine, jnp.tile(gain[None, :].astype(BF16), (1, 16)), jnp.zeros((), BF16))
-
-    return jnp.concatenate([gain_row(gain_attn), gain_row(gain_ffn), jnp.zeros((30, 512), BF16)], axis=0)
+    )(inputs, lengths, *weights, proj)
 
 
 def gelu_parts(x):
@@ -576,8 +570,8 @@
 
     def begin(self):
         pc = self.pc
-        for col in (pc.diag, pc.second, pc.first, pc.d):
-            for k in (1, 2, 3, 0):
+        for k in (1, 2, 3, 0):
+            for col in (pc.diag, pc.second, pc.first, pc.d):
                 self.to_sibling(col * 4 + lax.rem(pc.z + k, 4)).start()
 
     def pair(self, g):
@@ -799,52 +793,74 @@
                 rbuf[l, p] = tl.astype(BF16)
                 chain(l, p).start()
 
-            @pl.when((z == 2) & (p >= 3))
-            def _():
-                pass_on(p - 3)
-
             return 0
 
         lax.fori_loop(0, 4, tail_pair, 0)
         done(l, "att", "rden")
         needs(l, "sin", "fk", "vext", "pb", "wqk")
 
-        def attend_pair(p, _):
-            at_point("attend", p)
+        def of_head(h, value):
+            keep = lane_low(value.shape) if h == 0 else jnp.logical_not(lane_low(value.shape))
+            return jnp.where(keep, value, jnp.zeros((), BF16))
+
+        def through_lift(p, k, e):
+            gw = dot_nt(jnp.concatenate(e, axis=1), pb[p])
+            gw = gw[:, 0:128] + 2.0 * wqk[k, p].astype(F32) * gw[:, 128:256]
+            return (gw * scale).astype(BF16)
+
+        def query_pair(p, _):
+            at_point("query", p)
             at = pl.ds(pl.multiple_of(p * 128, 128), 128)
 
-            @pl.when((z == 2) & (p < 3))
+            @pl.when((z == 2) & (p >= 1))
             def _():
-                pass_on(p + 1)
+                pass_on(p - 1)
 
             ve = vext[p]
             lep = le[p]
-            dq, dk, dv = [], [], []
+            dq = []
             for h in (0, 1):
-                if h == 1:
-                    @pl.when(z == 1)
-                    def _():
-                        pass_on(p)
-
                 fl = slice(256 * h, 256 * h + 256)
-                keep = lane_low((512, 256)) if h == 0 else jnp.logical_not(lane_low((512, 256)))
-                leh = jnp.where(keep, lep, jnp.zeros((), BF16))
-                fqh, fkh = fq[p, :, fl], fk[p, :, fl]
+                leh = of_head(h, lep)
+                fkh = fk[p, :, fl]
                 zrow = sin[p, 128:144, :].astype(F32)[8 * h : 8 * h + 1, :]
                 st = jnp.concatenate([sin[p, 0:128, :], jnp.broadcast_to(zrow, (128, 256)).astype(BF16)], axis=0)
                 dqh = head_col * dot(leh, st)
                 da0 = dot_nt(leh[0:256], ve[0:256]).astype(BF16) * mask[0:256, 0:256]
                 da1 = dot_nt(leh[256:512], ve).astype(BF16) * mask[256:512, :]
                 dqh = dqh + jnp.concatenate([dot(da0, fkh[0:256]), dot(da1, fkh)], axis=0)
+                dq.append((dqh * fq[p, :, fl].astype(F32)).astype(BF16))
+            gq[:, at] = through_lift(p, 0, dq)
+            return 0
+
+        lax.fori_loop(0, 4, query_pair, 0)
+
+        def attend_pair(p, _):
+            at_point("attend", p)
+            at = pl.ds(pl.multiple_of(p * 128, 128), 128)
+
+            @pl.when((z == 2) & (p == 0))
+            def _():
+                pass_on(3)
+
+            ve = vext[p]
+            lep = le[p]
+            dk, dv = [], []
+            for h in (0, 1):
+                if h == 1:
+                    @pl.when(z == 1)
+                    def _():
+                        pass_on(p)
+
+                fl = slice(256 * h, 256 * h + 256)
+                leh = of_head(h, lep)
+                fqh, fkh = fq[p, :, fl], fk[p, :, fl]
                 at0 = dot_nt(fkh[0:256], fqh).astype(BF16) * mask_t[0:256, :]
                 at1 = dot_nt(fkh[256:512], fqh[256:512]).astype(BF16) * mask_t[256:512, 256:512]
-                dvh = jnp.concatenate([dot(at0, lep[:, 0:128]), dot(at1, lep[256:512, 0:128])], axis=0)
+                dv.append(jnp.concatenate([dot(at0, lep[:, 0:128]), dot(at1, lep[256:512, 0:128])], axis=0))
                 dt0 = dot_nt(ve[0:256], leh).astype(BF16) * mask_t[0:256, :]
                 dt1 = dot_nt(ve[256:512], leh[256:512]).astype(BF16) * mask_t[256:512, 256:512]
-                dkh = jnp.concatenate([dot(dt0, fqh), dot(dt1, fqh[256:512])], axis=0)
-                dq.append((dqh * fqh.astype(F32)).astype(BF16))
-                dk.append(dkh)
-                dv.append(dvh)
+                dk.append(jnp.concatenate([dot(dt0, fqh), dot(dt1, fqh[256:512])], axis=0))
 
             @pl.when(z == 0)
             def _():
@@ -859,10 +875,7 @@
                 dv[h] = dv[h] + tail_col * dot_nt(fkh, rin[l, p, 0:128, :])
                 dk[h] = ((dk[h] + tail_col * dot(ve, rte)) * fkh.astype(F32)).astype(BF16)
             gv[:, at] = jnp.where(low, dv[0], dv[1]).astype(BF16)
-            for k, e, out in ((0, dq, gq), (1, dk, gk)):
-                gw = dot_nt(jnp.concatenate(e, axis=1), pb[p])
-                gw = gw[:, 0:128] + 2.0 * wqk[k, p].astype(F32) * gw[:, 128:256]
-                out[:, at] = (gw * scale).astype(BF16)
+            gk[:, at] = through_lift(p, 1, dk)
             return 0
 
         lax.fori_loop(0, 4, attend_pair, 0)
@@ -908,13 +921,34 @@
         for k in (1, 2, 3, 0):
             m.stage3(k)
 
-    layer(1, {"tail": lambda p: sums[1, 0].stage1(0, p), "attend": lambda p: sums[1, 0].stage1(1, p),
-              "norm": sums[1, 0].stage2})
-    along_z(sums[1, 0])
-    layer(0, {"ffn": lambda p: (sums[1, 1].stage1(0, p), sums[1, 1].stage1(1, p)), "branch": sums[1, 1].stage2,
-              "middle": lambda: along_z(sums[1, 1]),
-              "tail": lambda p: sums[0, 0].stage1(0, p), "attend": lambda p: sums[0, 0].stage1(1, p),
-              "norm": sums[0, 0].stage2, "out": lambda i: (sums[0, 1].stage1(0, i), sums[0, 1].stage1(1, i))})
+    def both(m):
+        return lambda i: (m.stage1(0, i), m.stage1(1, i))
+
+    def at_steps(**steps):
+        def run(i):
+            for name, step in steps.items():
+                pl.when(i == int(name[1:]))(step)
+
+        return run
+
+    def larger(l, extra=lambda: None):
+        m = sums[l, 0]
+        return {
+            "tail": both(m),
+            "attend": at_steps(i1=lambda: m.stage2(0), i3=lambda: (m.stage2(1), extra())[0]),
+            "norm": at_steps(i0=lambda: m.stage3(1), i3=lambda: m.stage2(2)),
+            "late": lambda: m.stage3(2),
+            "out": at_steps(i1=lambda: m.stage2(3)),
+        }
+
+    m1, m0 = sums[1, 0], sums[0, 0]
+    layer(1, {"tail": both(m1), "attend": at_steps(i1=lambda: m1.stage2(0), i3=lambda: m1.stage2(1)),
+              "norm": at_steps(i3=lambda: m1.stage2(2)), "out": at_steps(i1=lambda: m1.stage2(3), i3=lambda: m1.stage3(1))})
+    early = at_steps(i0=lambda: m1.stage3(2), i1=lambda: m1.stage3(3), i2=lambda: m1.stage3(0))
+    hooks = larger(0, lambda: four(sums[1, 1].stage2))
+    late_steps = hooks["out"]
+    hooks["out"] = lambda i: (both(sums[0, 1])(i), late_steps(i))
+    layer(0, {"ffn": lambda i: (early(i), both(sums[1, 1])(i)), **hooks})
     own_act = pltpu.make_async_copy(xout.at[c], gin.at[c], asem.at[0])
     own_act.start()
     far_act = remote(xout.at[pc.o], gin.at[c], asem.at[1], asem.at[2], pc.sibling())
@@ -922,7 +956,9 @@
     own_act.wait()
     far_act.wait()
 
-    along_z(sums[0, 0])
+    along_z(sums[1, 1])
+    sums[0, 0].stage3(3)
+    sums[0, 0].stage3(0)
     four(sums[0, 1].stage2)
     along_z(sums[0, 1])
     for m in sums.values():
@@ -1014,20 +1050,39 @@
     )(cotangent, lengths, *weights, *saved)
 
 
+def finish_kernel(*refs):
+    n = len(refs) // 2
+    ins, outs, sems = refs[:n], refs[n : 2 * n - 1], refs[2 * n - 1 :]
+    sums, ga, gf = ins[n - 3 :]
+    copies = [pltpu.make_async_copy(src, dst, sems[0].at[i]) for i, (src, dst) in enumerate(zip(ins[: n - 3], outs))]
+    for copy in copies:
+        copy.start()
+    for i, gain in ((0, ga), (1, gf)):
+        outs[n - 3 + i][...] = sums[i].T[0:1, 0:32] / gain[...].astype(BF16).astype(F32)
+    for copy in copies:
+        copy.wait()
+
+
+def finish_call(results, sums, gain_attn, gain_ffn):
+    vm = pl.BlockSpec(memory_space=pltpu.VMEM)
+    hbm = pl.BlockSpec(memory_space=pl.ANY)
+    n = len(results)
+    return pl.pallas_call(
+        finish_kernel,
+        out_shape=[jax.ShapeDtypeStruct(r.shape, r.dtype) for r in results + [gain_attn, gain_ffn]],
+        in_specs=[hbm] * n + [vm] * 3,
+        out_specs=[vm] * (n + 2),
+        scratch_shapes=[pltpu.SemaphoreType.DMA((n,))],
+        name="finish",
+    )(*results, sums, gain_attn, gain_ffn)
+
+
 def fast_local(inputs, cotangent, doc_lengths, feature_proj, *weights):
-    gain_rows = make_gain_rows(weights[6][0], weights[7][0])
-    outs = forward_call(inputs, doc_lengths, weights[:6], gain_rows, feature_proj)
+    act, *saved = forward_call(inputs, doc_lengths, weights, feature_proj)
     w_query, w_key, w_value, _, w_up = weights[:5]
-    gin, *grads = backward_call(cotangent, doc_lengths, (w_query, w_key, w_value, w_up), outs[1:])
-
-    def by_gain(sums, gain):
-        return sums[None, :, 0] / gain.astype(BF16).astype(F32)
-
-    return (
-        (outs[0][None, :, None], gin[None, :, None])
-        + tuple(g[None] for g in grads[:6])
-        + (by_gain(grads[6][0], weights[6]), by_gain(grads[6][1], weights[7]))
-    )
+    gin, *grads = backward_call(cotangent, doc_lengths, (w_query, w_key, w_value, w_up), saved)
+    done = finish_call([act, gin] + grads[:6], grads[6], weights[6], weights[7])
+    return (done[0][None, :, None], done[1][None, :, None]) + tuple(g[None] for g in done[2:8]) + tuple(done[8:])
 
 
 HIGH_PRECISION = lax.Precision.HIGHEST

time: 214 us -> 201 us (0.939)
  local copies, waits for them, and re-layouts: 8.56 us -> 0 us
  other arithmetic: 3.06 us -> 0 us
    unnamed x26 -> x0, local copies, waits for them, and re-layouts: 7.25 us -> none
    pallas_call x1, Pallas kernels: 103 us -> 97.5 us  [backward_call(): pl.pallas_call(backward_kernel, out_shape=[sds((2, 512, 512), BF16)] + [s...]
    pallas_call x0 -> x1, Pallas kernels: none -> 4.17 us  [finish_call(): pl.pallas_call(finish_kernel, out_shape=[jax.ShapeDtypeStruct(r.shape, r....]
where the time goes in v3:
time: 201 us; the launch traced here: 200 us
  Pallas kernels  199 us (99%)
    pallas_call x1, Pallas kernels, forward_call(): pl.pallas_call(forward_kernel, out_shape=[sds((2, 512, 512), BF16)] + sav...  97.8 us
    pallas_call x1, Pallas kernels, backward_call(): pl.pallas_call(backward_kernel, out_shape=[sds((2, 512, 512), BF16)] + [s...  97.5 us
    pallas_call x1, Pallas kernels, finish_call(): pl.pallas_call(finish_kernel, out_shape=[jax.ShapeDtypeStruct(r.shape, r....  4.17 us

profile of v3, /device:TPU:27, one launch (start us, length us, event | category | flops | bytes accessed | tf_op | source)
XLA Modules:
  0.0 200.3 jit_solution(7328598044768116328)
XLA Ops:
  0.6 97.8 %forward.1 = (bf16[2,512,512]{2,1,0:T(8,128)(2,1)}, bf16[2,16,416,512]{3,2,1,0:T(8,128)(2,1)}, bf16[2,4,512,512]{3,2,1,0:T(8,128)(2,1)}, bf16[2,4,512,512]{3,2,1...) custom-call(bf16[2,1,512,512]{3,2,1,0:T(8,128)(2,1)} %inputs.1, ...), custom_call_target="tpu_custom_call" | custom-call | tf_op jit(solution)/shard_map/forward/pallas_call | solution.py:510
  98.4 97.5 %backward.1 = (bf16[2,512,512]{2,1,0:T(8,128)(2,1)}, f32[32,512]{1,0:T(8,128)}, f32[32,512]{1,0:T(8,128)}, f32[32,512]{1,0:T(8,128)}, f32[32,512]{1,0:T(8,128)},...) custom-call(bf16[2,1,512,512]{3,2,1,0:T(8,128)(2,1)} %cotangent.1, s32[2,1,4]{2,1,0:T(1,128)} %lengths.3, ...), custom_call_target="tpu_custom_call" | custom-call | tf_op jit(solution)/shard_map/backward/pallas_call | solution.py:1038
  196.0 4.2 %finish.1 = (bf16[2,512,512]{2,1,0:T(8,128)(2,1)}, bf16[2,512,512]{2,1,0:T(8,128)(2,1)}, f32[32,512]{1,0:T(8,128)}, f32[32,512]{1,0:T(8,128)}, f32[32,512]{1,0:T...) custom-call(bf16[2,512,512]{2,1,0:T(8,128)(2,1)} %get-tuple-element., ...), custom_call_target="tpu_custom_call" | custom-call | tf_op jit(solution)/shard_map/finish/pallas_call | solution.py:1070

commit v4 on v3

--- a/solution.py
+++ b/solution.py
@@ -12,8 +12,8 @@
 BF16 = jnp.bfloat16
 VMEM_LIMIT = 63 << 20
 
-ROW_Q, ROW_K, ROW_V, ROW_O, ROW_UP, ROW_DOWN, SLAB = 32, 64, 96, 128, 160, 288, 416
-PORTIONS = ((0, 64), (128, 144))
+ROW_Q, ROW_K, ROW_V, ROW_O, ROW_UP, ROW_DOWN, SLAB = 0, 32, 64, 96, 128, 256, 384
+PORTIONS = ((0, 48), (96, 144))
 
 
 def dot(a, b):
@@ -70,10 +70,11 @@
 
 
 class Gather:
-    def __init__(self, pc, G, l, por, ssem, rsem, dsend, drecv):
+    def __init__(self, pc, G, l, por, ssem, rsem, dsend, drecv, tiles=None):
         base, self.n = PORTIONS[por]
         self.pc, self.G, self.l, self.por = pc, G, l, por
         self.sems = ssem, rsem, dsend, drecv
+        self.tiles = tiles
         self.start = pl.multiple_of(base + pc.c * self.n, 16)
         self.other = pl.multiple_of(base + pc.o * self.n, 16)
 
@@ -83,6 +84,15 @@
     def link(self, g, i, dev):
         ssem, rsem, _, _ = self.sems
         return remote(self.ref(g), self.ref(g), ssem.at[self.l, self.por, i], rsem.at[self.l, self.por, g], dev)
+
+    def tile(self, g, i, dev):
+        ref, tsend, trecv = self.tiles
+        return remote(ref.at[g], ref.at[g], tsend.at[i], trecv.at[g], dev)
+
+    def pass_to(self, g, i, dev):
+        self.link(g, i, dev).start()
+        if self.tiles:
+            self.tile(g, i, dev).start()
 
     def sib(self, g):
         _, _, dsend, drecv = self.sems
@@ -92,13 +102,15 @@
 
     def arrive(self, g):
         self.link(g, 0, self.pc.sibling()).wait_recv()
+        if self.tiles:
+            self.tile(g, 0, self.pc.sibling()).wait_recv()
 
     def own(self):
         pc = self.pc
         for k in (2, 1, 3):
-            self.link(pc.me, k, pc.at(pc.d, lax.rem(pc.z + k, 4))).start()
-        self.link(pc.me, 4, pc.at(pc.first, pc.z)).start()
-        self.link(pc.me, 8, pc.at(pc.second, pc.z)).start()
+            self.pass_to(pc.me, k, pc.at(pc.d, lax.rem(pc.z + k, 4)))
+        self.pass_to(pc.me, 4, pc.at(pc.first, pc.z))
+        self.pass_to(pc.me, 8, pc.at(pc.second, pc.z))
 
     def column(self, k):
         pc = self.pc
@@ -106,8 +118,8 @@
         def step():
             g = pc.d * 4 + lax.rem(pc.z + k, 4)
             self.arrive(g)
-            self.link(g, 4 + k, pc.at(pc.first, pc.z)).start()
-            self.link(g, 8 + k, pc.at(pc.second, pc.z)).start()
+            self.pass_to(g, 4 + k, pc.at(pc.first, pc.z))
+            self.pass_to(g, 8 + k, pc.at(pc.second, pc.z))
             self.sib(g).start()
 
         if not isinstance(k, int):
@@ -119,7 +131,7 @@
         pc = self.pc
         g = pc.first * 4 + lax.rem(pc.z + k, 4)
         self.arrive(g)
-        self.link(g, 12 + k, pc.at(pc.second, pc.z)).start()
+        self.pass_to(g, 12 + k, pc.at(pc.second, pc.z))
         self.sib(g).start()
 
     def far(self, k):
@@ -149,6 +161,8 @@
 
         def step(i, _):
             self.link(pc.me, 1 + i, pc.at(pc.first, pc.z)).wait_send()
+            if self.tiles:
+                self.tile(pc.me, 1 + i, pc.at(pc.first, pc.z)).wait_send()
             self.sib(lax.rem(pc.me + 1 + i, 16)).wait_send()
             return 0
 
@@ -187,20 +201,19 @@
 
 def forward_kernel(
     inputs, lengths, wq_in, wk_in, wv_in, wo_in, wup_in, wdown_in, ga_in, gf_in, proj,
-    act, G_out, fq_out, fk_out, v_out, att_out, rden_out, branch_out, w_out, x_out, sin_out, pb_out,
+    act, G_out, fq_out, fk_out, v_out, att_out, rden_out, branch_out, w_out, x_out, sin_out, pb_out, gains_out,
     G, px, pk, mask, xbuf, hbuf, qbuf, kbuf, fq, fk, vext, att, rden, branch, wqk, xin, sin, tail, sbuf,
-    gains, ybuf, hf, acc,
-    ssem, rsem, dsend, drecv, osem, osem2, psem, csend, crecv, asem, wsem,
+    gains, ybuf, hf, acc, tile_a, tile_b, tiles,
+    ssem, rsem, dsend, drecv, osem, osem2, psem, csend, crecv, asem, wsem, gsend, grecv,
 ):
     pc = Place()
     c, z = pc.c, pc.z
     pc.greet()
-    gains[...] = jnp.zeros_like(gains)
-    gains[0:1, 0:32] = ga_in[...]
-    gains[1:2, 0:32] = gf_in[...]
-    placed = pltpu.roll(gains[0:8, :], 32 * pc.me, 1)
-    G[c, pc.me, 0:16, :] = jnp.concatenate([placed, jnp.zeros((8, 512), F32)], axis=0).astype(BF16)
-    G[c, pc.me, 16:ROW_Q, :] = jnp.zeros((ROW_Q - 16, 512), BF16)
+    tile_a[...] = jnp.zeros_like(tile_a)
+    tile_a[0:1, 0:32] = ga_in[...]
+    tile_a[1:2, 0:32] = gf_in[...]
+    placed = pltpu.roll(pltpu.roll(tile_a[...], 32 * z, 1), 2 * c, 0)
+    tile_b[0] = placed.astype(BF16)
     for ref, row in ((wq_in, ROW_Q), (wk_in, ROW_K), (wv_in, ROW_V), (wo_in, ROW_O)):
         G[c, pc.me, row : row + 32, :] = ref[0].astype(BF16)
     for j in range(4):
@@ -217,10 +230,16 @@
             ref = G.at[c, pc.me, pl.ds(pl.multiple_of(base + at * n, 16), n)]
             halves[por, half] = remote(ref, ref, osem2.at[0, por, half], osem2.at[1, por, half], pc.sibling())
             halves[por, half].start()
+    tsend = remote(tile_b.at[0], tile_b.at[1], psem.at[2], psem.at[3], pc.sibling())
+    tsend.start()
     psend = remote(px.at[c], px.at[c], psem.at[0], psem.at[1], pc.sibling())
     psend.start()
     moves = {
-        (l, por): Gather(pc, G, l, por, ssem, rsem, dsend, drecv) for l in (0, 1) for por in range(2)
+        (l, por): Gather(
+            pc, G, l, por, ssem, rsem, dsend, drecv, (tiles, gsend, grecv) if l == 0 and por == 0 else None
+        )
+        for l in (0, 1)
+        for por in range(2)
     }
 
     def four(step):
@@ -230,6 +249,8 @@
     for por in (0, 1):
         for half in (0, 1):
             halves[por, half].wait()
+    tsend.wait()
+    tiles[pc.me] = (tile_b[0].astype(F32) + tile_b[1].astype(F32)).astype(BF16)
     moves[0, 0].own()
 
     first_row = z * 512
@@ -274,6 +295,9 @@
     four(moves[0, 0].far)
     four(moves[0, 1].across)
     moves[0, 0].finish()
+    for dp in range(4):
+        gains[:, 128 * dp : 128 * dp + 128] = jnp.sum(tiles[4 * dp : 4 * dp + 4].astype(F32), axis=0)
+    gains_out[...] = gains[...]
     below = (c, pc.d, jnp.minimum(z + 1, 3))
     low = lane_low((512, 128))
     row_low = lax.broadcasted_iota(jnp.int32, (144, 256), 0)
@@ -304,13 +328,11 @@
         pl.when(c != l)(lambda: give_far(l).start())
 
     def layer(l, during):
-        gains[...] = jnp.sum(G[l, :, 0:16, :].astype(F32), axis=0)
-
         def norm_tile(i, _):
             at = pl.ds(pl.multiple_of(i * 128, 128), 128)
             x = xbuf[at, :]
             xin[l, at, :] = x.astype(BF16)
-            hbuf[at, :] = (norm(x)[0] * gains[0:1, :]).astype(BF16)
+            hbuf[at, :] = (norm(x)[0] * gains[2 * l : 2 * l + 1, :]).astype(BF16)
             return 0
 
         lax.fori_loop(0, 4, norm_tile, 0)
@@ -416,7 +438,7 @@
             at = pl.ds(pl.multiple_of(i * 256, 256), 256)
             b = xbuf[at, :] + dot(att[l, at, :].astype(BF16), weight(G, l, ROW_O))
             branch[l, at, :] = b
-            hf[at, :] = (norm(b)[0] * gains[1:2, :]).astype(BF16)
+            hf[at, :] = (norm(b)[0] * gains[2 * l + 1 : 2 * l + 2, :]).astype(BF16)
             acc[at, :] = b
             return 0
 
@@ -478,7 +500,7 @@
         sds((2, 16, SLAB, 512), BF16), sds((2, 4, 512, 512), BF16), sds((2, 4, 512, 512), BF16),
         sds((2, 4, 512, 256), BF16), sds((2, 512, 512), F32), sds((2, 512, 512), F32), sds((2, 512, 512), F32),
         sds((2, 2, 4, 512, 128), BF16), sds((2, 512, 512), BF16), sds((2, 4, 144, 256), BF16),
-        sds((2, 4, 256, 512), BF16),
+        sds((2, 4, 256, 512), BF16), sds((16, 512), F32),
     ]
     scratch = [
         pltpu.VMEM((2, 16, SLAB, 512), BF16),
@@ -504,14 +526,17 @@
         pltpu.VMEM((2, 512, 512), BF16),
         pltpu.VMEM((512, 512), BF16),
         pltpu.VMEM((512, 512), F32),
-        dma((2, 2, 16)), dma((2, 2, 16)), dma((2, 2, 16)), dma((2, 2, 16)), dma, dma((2, 2, 2)), dma((2,)),
-        dma((2, 4)), dma((2, 4)), dma((3,)), dma((2, 10)),
+        pltpu.VMEM((16, 128), F32),
+        pltpu.VMEM((2, 16, 128), BF16),
+        pltpu.VMEM((16, 16, 128), BF16),
+        dma((2, 2, 16)), dma((2, 2, 16)), dma((2, 2, 16)), dma((2, 2, 16)), dma, dma((2, 2, 2)), dma((4,)),
+        dma((2, 4)), dma((2, 4)), dma((3,)), dma((2, 10)), dma((16,)), dma((16,)),
     ]
     return pl.pallas_call(
         forward_kernel,
         out_shape=[sds((2, 512, 512), BF16)] + saved,
         in_specs=[vm, pl.BlockSpec(memory_space=pltpu.SMEM)] + [vm] * 9,
-        out_specs=[vm] + [hbm] * len(saved),
+        out_specs=[vm] + [hbm] * (len(saved) - 1) + [vm],
         scratch_shapes=scratch,
         compiler_params=pltpu.CompilerParams(
             collective_id=0, has_side_effects=True, vmem_limit_bytes=VMEM_LIMIT
@@ -633,7 +658,7 @@
 
 
 def backward_kernel(
-    cotangent, lengths, wq_in, wk_in, wv_in, wup_in, G_in, fq_in, fk_in, v_in, att_in, rden_in, branch_in, w_in, x_in, sin_in, pb_in,
+    cotangent, lengths, wq_in, wk_in, wv_in, wup_in, G_in, fq_in, fk_in, v_in, att_in, rden_in, branch_in, w_in, x_in, sin_in, pb_in, gains_in,
     gin, gq_out, gk_out, gv_out, go_out, gup_out, gdown_out, gg_out,
     G, fq, fk, vext, att, rden, branch, wqk, xin, sin, pb,
     mask, mask_t, gbuf, gbr, hbuf, hT, gb, dh, gq, gk, gv, le, rin, rtail, rbuf, gains, xout, slabs,
@@ -642,10 +667,9 @@
 ):
     pc = Place()
     c, z = pc.c, pc.z
-    top, attn, ffn = pl.ds(0, 16), pl.ds(ROW_Q, ROW_UP - ROW_Q), pl.ds(ROW_UP, SLAB - ROW_UP)
+    attn, ffn = pl.ds(ROW_Q, ROW_UP - ROW_Q), pl.ds(ROW_UP, SLAB - ROW_UP)
     loads = {
-        "branch": (lambda l: branch_in.at[l], branch), "top": (lambda l: G_in.at[l, :, top], G.at[:, top]),
-        "ffn": (lambda l: G_in.at[l, :, ffn], G.at[:, ffn]), "att": (lambda l: att_in.at[l], att),
+        "branch": (lambda l: branch_in.at[l], branch),         "ffn": (lambda l: G_in.at[l, :, ffn], G.at[:, ffn]), "att": (lambda l: att_in.at[l], att),
         "attn": (lambda l: G_in.at[l, :, attn], G.at[:, attn]), "rden": (lambda l: rden_in.at[l], rden),
         "fq": (lambda l: fq_in.at[l], fq), "sin": (lambda l: sin_in.at[l], sin), "fk": (lambda l: fk_in.at[l], fk),
         "vext": (lambda l: v_in.at[l], vext), "pb": (lambda l: pb_in.at[l], pb), "wqk": (lambda l: w_in.at[l], wqk),
@@ -666,6 +690,7 @@
                 load(0, name).start()
 
     pc.greet()
+    gains[...] = gains_in[...]
     for name in loads:
         load(1, name).start()
 
@@ -714,12 +739,11 @@
             if name in during:
                 during[name](*args)
 
-        needs(l, "branch", "top")
-        gains[...] = jnp.sum(G[:, 0:16, :].astype(F32), axis=0)
+        needs(l, "branch")
 
         def norm_tile(i, _):
             at = pl.ds(pl.multiple_of(i * 128, 128), 128)
-            hbuf[at, :] = (norm(branch[at, :])[0] * gains[1:2, :]).astype(BF16)
+            hbuf[at, :] = (norm(branch[at, :])[0] * gains[2 * l + 1 : 2 * l + 2, :]).astype(BF16)
             gb[at, :] = gbuf[at, :].astype(BF16)
             return 0
 
@@ -745,7 +769,7 @@
 
         needs(l, "ffn")
         lax.fori_loop(0, 4, ffn_tile, 0)
-        done(l, "top", "ffn")
+        done(l, "ffn")
         needs(l, "att")
 
         def branch_tile(i, _):
@@ -753,7 +777,7 @@
             at = pl.ds(pl.multiple_of(i * 128, 128), 128)
             y, rstd = norm(branch[at, :])
             d = dh[at, :]
-            g = gbuf[at, :] + norm_back(y, rstd, d * gains[1:2, :])
+            g = gbuf[at, :] + norm_back(y, rstd, d * gains[2 * l + 1 : 2 * l + 2, :])
             gbr[at, :] = g
             gb[at, :] = g.astype(BF16)
             hbuf[at, :] = att[at, :].astype(BF16)
@@ -885,7 +909,7 @@
         def norm_tile2(i, _):
             at_point("norm", i)
             at = pl.ds(pl.multiple_of(i * 128, 128), 128)
-            hbuf[at, :] = (norm(xin[at, :].astype(F32))[0] * gains[0:1, :]).astype(BF16)
+            hbuf[at, :] = (norm(xin[at, :].astype(F32))[0] * gains[2 * l : 2 * l + 1, :]).astype(BF16)
             return 0
 
         lax.fori_loop(0, 4, norm_tile2, 0)
@@ -905,7 +929,7 @@
             at = pl.ds(pl.multiple_of(i * 128, 128), 128)
             y, rstd = norm(xin[at, :].astype(F32))
             d = dh[at, :]
-            g = (gbr[at, :] + norm_back(y, rstd, d * gains[0:1, :])).astype(BF16)
+            g = (gbr[at, :] + norm_back(y, rstd, d * gains[2 * l : 2 * l + 1, :])).astype(BF16)
             xout[l, at, :] = g
             gbuf[at, :] = g.astype(F32)
             return 0
@@ -1006,7 +1030,7 @@
     dma = pltpu.SemaphoreType.DMA
     vm = pl.BlockSpec(memory_space=pltpu.VMEM)
     hbm = pl.BlockSpec(memory_space=pl.ANY)
-    bufs = [pltpu.VMEM(a.shape[1:], a.dtype) for a in saved]
+    bufs = [pltpu.VMEM(a.shape[1:], a.dtype) for a in saved[:-1]]
     full = (512, 512)
     scratch = bufs + [
         pltpu.VMEM(full, BF16),
@@ -1040,7 +1064,7 @@
         out_shape=[sds((2, 512, 512), BF16)]
         + [sds((32, 512), F32)] * 4
         + [sds((32, 2048), F32), sds((128, 512), F32), sds((2, 32, 128), F32)],
-        in_specs=[vm, pl.BlockSpec(memory_space=pltpu.SMEM)] + [vm] * 4 + [hbm] * len(saved),
+        in_specs=[vm, pl.BlockSpec(memory_space=pltpu.SMEM)] + [vm] * 4 + [hbm] * (len(saved) - 1) + [vm],
         out_specs=[vm] * 8,
         scratch_shapes=scratch,
         compiler_params=pltpu.CompilerParams(

time: 201 us -> 198 us (0.985)
    pallas_call x1, Pallas kernels: 97.8 us -> 95.3 us  [forward_call(): pl.pallas_call(forward_kernel, out_shape=[sds((2, 512, 512), BF16)] + sav...]
where the time goes in v4:
time: 198 us
  Pallas kernels  197 us (99%)
    pallas_call x1, Pallas kernels, backward_call(): pl.pallas_call(backward_kernel, out_shape=[sds((2, 512, 512), BF16)] + [s...  97.4 us
    pallas_call x1, Pallas kernels, forward_call(): pl.pallas_call(forward_kernel, out_shape=[sds((2, 512, 512), BF16)] + sav...  95.3 us
    pallas_call x1, Pallas kernels, finish_call(): pl.pallas_call(finish_kernel, out_shape=[jax.ShapeDtypeStruct(r.shape, r....  4.17 us

profile of v4, /device:TPU:27, one launch (start us, length us, event | category | flops | bytes accessed | tf_op | source)
XLA Modules:
  0.0 197.7 jit_solution(11732164295295605194)
XLA Ops:
  0.6 95.3 %forward.1 = (bf16[2,512,512]{2,1,0:T(8,128)(2,1)}, bf16[2,16,384,512]{3,2,1,0:T(8,128)(2,1)}, bf16[2,4,512,512]{3,2,1,0:T(8,128)(2,1)}, bf16[2,4,512,512]{3,2,1...) custom-call(bf16[2,1,512,512]{3,2,1,0:T(8,128)(2,1)} %inputs.1, ...), custom_call_target="tpu_custom_call" | custom-call | tf_op jit(solution)/shard_map/forward/pallas_call | solution.py:535
  96.0 97.4 %backward.1 = (bf16[2,512,512]{2,1,0:T(8,128)(2,1)}, f32[32,512]{1,0:T(8,128)}, f32[32,512]{1,0:T(8,128)}, f32[32,512]{1,0:T(8,128)}, f32[32,512]{1,0:T(8,128)},...) custom-call(bf16[2,1,512,512]{3,2,1,0:T(8,128)(2,1)} %cotangent.1, s32[2,1,4]{2,1,0:T(1,128)} %lengths.3, ...), custom_call_target="tpu_custom_call" | custom-call | tf_op jit(solution)/shard_map/backward/pallas_call | solution.py:1062
  193.4 4.2 %finish.1 = (bf16[2,512,512]{2,1,0:T(8,128)(2,1)}, bf16[2,512,512]{2,1,0:T(8,128)(2,1)}, f32[32,512]{1,0:T(8,128)}, f32[32,512]{1,0:T(8,128)}, f32[32,512]{1,0:T...) custom-call(bf16[2,512,512]{2,1,0:T(8,128)(2,1)} %get-tuple-element., ...), custom_call_target="tpu_custom_call" | custom-call | tf_op jit(solution)/shard_map/finish/pallas_call | solution.py:1094

commit v5 on v4

--- a/solution.py
+++ b/solution.py
@@ -69,6 +69,10 @@
     return G[l, :, row : row + n, :].reshape(16 * n, 512)
 
 
+def nearest(k):
+    return k + (k // 2 if isinstance(k, int) else lax.div(k, 2)) * (5 - 2 * k)
+
+
 class Gather:
     def __init__(self, pc, G, l, por, ssem, rsem, dsend, drecv, tiles=None):
         base, self.n = PORTIONS[por]
@@ -107,7 +111,7 @@
 
     def own(self):
         pc = self.pc
-        for k in (2, 1, 3):
+        for k in (1, 3, 2):
             self.pass_to(pc.me, k, pc.at(pc.d, lax.rem(pc.z + k, 4)))
         self.pass_to(pc.me, 4, pc.at(pc.first, pc.z))
         self.pass_to(pc.me, 8, pc.at(pc.second, pc.z))
@@ -116,7 +120,7 @@
         pc = self.pc
 
         def step():
-            g = pc.d * 4 + lax.rem(pc.z + k, 4)
+            g = pc.d * 4 + lax.rem(pc.z + nearest(k), 4)
             self.arrive(g)
             self.pass_to(g, 4 + k, pc.at(pc.first, pc.z))
             self.pass_to(g, 8 + k, pc.at(pc.second, pc.z))
@@ -129,14 +133,14 @@
 
     def across(self, k):
         pc = self.pc
-        g = pc.first * 4 + lax.rem(pc.z + k, 4)
+        g = pc.first * 4 + lax.rem(pc.z + nearest(k), 4)
         self.arrive(g)
         self.pass_to(g, 12 + k, pc.at(pc.second, pc.z))
         self.sib(g).start()
 
     def far(self, k):
         pc = self.pc
-        zz = lax.rem(pc.z + k, 4)
+        zz = lax.rem(pc.z + nearest(k), 4)
         for dp in (pc.second, pc.diag):
             g = dp * 4 + zz
             self.arrive(g)
@@ -466,10 +470,13 @@
 
     def before_branch(l):
         if l == 0:
-            four(moves[0, 1].far)
+            four(moves[1, 0].across)
+        else:
+            for key in ((0, 0), (0, 1), (1, 0)):
+                moves[key].drain()
         moves[l, 1].finish()
 
-    layer(0, {"key": moves[1, 0].column, "query": moves[1, 1].column, "attend": moves[1, 0].across,
+    layer(0, {"key": moves[1, 0].column, "query": moves[1, 1].column, "attend": moves[0, 1].far,
               "branch": lambda: before_branch(0), "ffn": moves[1, 1].across})
     four(moves[1, 0].far)
     moves[1, 0].finish()
@@ -487,8 +494,7 @@
             for p in range(4):
                 chain(l, p).wait_send()
 
-    for move in moves.values():
-        move.drain()
+    moves[1, 1].drain()
 
 
 def forward_call(inputs, lengths, weights, proj):
@@ -859,6 +865,15 @@
 
         lax.fori_loop(0, 4, query_pair, 0)
 
+        needs(l, "xin")
+
+        def norm_tile2(i, _):
+            at = pl.ds(pl.multiple_of(i * 128, 128), 128)
+            hbuf[at, :] = (norm(xin[at, :].astype(F32))[0] * gains[2 * l : 2 * l + 1, :]).astype(BF16)
+            return 0
+
+        lax.fori_loop(0, 4, norm_tile2, 0)
+        hT[...] = hbuf[...].T
         def attend_pair(p, _):
             at_point("attend", p)
             at = pl.ds(pl.multiple_of(p * 128, 128), 128)
@@ -904,16 +919,8 @@
 
         lax.fori_loop(0, 4, attend_pair, 0)
         done(l, "fq", "sin", "fk", "vext", "pb", "wqk")
-        needs(l, "xin")
-
-        def norm_tile2(i, _):
-            at_point("norm", i)
-            at = pl.ds(pl.multiple_of(i * 128, 128), 128)
-            hbuf[at, :] = (norm(xin[at, :].astype(F32))[0] * gains[2 * l : 2 * l + 1, :]).astype(BF16)
-            return 0
-
-        lax.fori_loop(0, 4, norm_tile2, 0)
-        hT[...] = hbuf[...].T
+
+        at_point("norm")
         for row, g in ((ROW_Q, gq), (ROW_K, gk), (ROW_V, gv)):
             put(l, row, 32, dot(hT[...], g[...]))
         sums[l, 1].begin()
@@ -959,15 +966,15 @@
         m = sums[l, 0]
         return {
             "tail": both(m),
-            "attend": at_steps(i1=lambda: m.stage2(0), i3=lambda: (m.stage2(1), extra())[0]),
-            "norm": at_steps(i0=lambda: m.stage3(1), i3=lambda: m.stage2(2)),
+            "attend": at_steps(i1=lambda: m.stage2(0), i2=lambda: m.stage2(1), i3=lambda: extra()),
+            "norm": lambda: (m.stage3(1), m.stage2(2)),
             "late": lambda: m.stage3(2),
             "out": at_steps(i1=lambda: m.stage2(3)),
         }
 
     m1, m0 = sums[1, 0], sums[0, 0]
     layer(1, {"tail": both(m1), "attend": at_steps(i1=lambda: m1.stage2(0), i3=lambda: m1.stage2(1)),
-              "norm": at_steps(i3=lambda: m1.stage2(2)), "out": at_steps(i1=lambda: m1.stage2(3), i3=lambda: m1.stage3(1))})
+              "norm": lambda: m1.stage2(2), "out": at_steps(i1=lambda: m1.stage2(3), i3=lambda: m1.stage3(1))})
     early = at_steps(i0=lambda: m1.stage3(2), i1=lambda: m1.stage3(3), i2=lambda: m1.stage3(0))
     hooks = larger(0, lambda: four(sums[1, 1].stage2))
     late_steps = hooks["out"]
@@ -981,6 +988,7 @@
     far_act.wait()
 
     along_z(sums[1, 1])
+    sums[1, 0].drain()
     sums[0, 0].stage3(3)
     sums[0, 0].stage3(0)
     four(sums[0, 1].stage2)
@@ -1015,8 +1023,8 @@
         gf = gf + up * total[ROW_UP + 32 * j : ROW_UP + 32 * j + 32, :]
     gg_out[0] = jnp.broadcast_to(jnp.sum(ga, axis=1, keepdims=True), (32, 128))
     gg_out[1] = jnp.broadcast_to(jnp.sum(gf, axis=1, keepdims=True), (32, 128))
-    for m in sums.values():
-        m.drain()
+    for key in ((1, 1), (0, 0), (0, 1)):
+        sums[key].drain()
 
     @pl.when(z > 0)
     def _():

time: 198 us -> 190 us (0.960)
  Pallas kernels: 197 us -> 187 us
    pallas_call x1, Pallas kernels: 95.3 us -> 87.6 us  [forward_call(): pl.pallas_call(forward_kernel, out_shape=[sds((2, 512, 512), BF16)] + sav...]
    pallas_call x1, Pallas kernels: 97.4 us -> 95.3 us  [backward_call(): pl.pallas_call(backward_kernel, out_shape=[sds((2, 512, 512), BF16)] + [s...]
where the time goes in v5:
time: 190 us; the launch traced here: 188 us
  Pallas kernels  187 us (98%)
    pallas_call x1, Pallas kernels, backward_call(): pl.pallas_call(backward_kernel, out_shape=[sds((2, 512, 512), BF16)] + [s...  95.3 us
    pallas_call x1, Pallas kernels, forward_call(): pl.pallas_call(forward_kernel, out_shape=[sds((2, 512, 512), BF16)] + sav...  87.6 us
    pallas_call x1, Pallas kernels, finish_call(): pl.pallas_call(finish_kernel, out_shape=[jax.ShapeDtypeStruct(r.shape, r....  4.17 us

profile of v5, /device:TPU:27, one launch (start us, length us, event | category | flops | bytes accessed | tf_op | source)
XLA Modules:
  0.0 188.0 jit_solution(7783149165856743249)
XLA Ops:
  0.6 87.6 %forward.1 = (bf16[2,512,512]{2,1,0:T(8,128)(2,1)}, bf16[2,16,384,512]{3,2,1,0:T(8,128)(2,1)}, bf16[2,4,512,512]{3,2,1,0:T(8,128)(2,1)}, bf16[2,4,512,512]{3,2,1...) custom-call(bf16[2,1,512,512]{3,2,1,0:T(8,128)(2,1)} %inputs.1, ...), custom_call_target="tpu_custom_call" | custom-call | tf_op jit(solution)/shard_map/forward/pallas_call | solution.py:541
  88.3 95.3 %backward.1 = (bf16[2,512,512]{2,1,0:T(8,128)(2,1)}, f32[32,512]{1,0:T(8,128)}, f32[32,512]{1,0:T(8,128)}, f32[32,512]{1,0:T(8,128)}, f32[32,512]{1,0:T(8,128)},...) custom-call(bf16[2,1,512,512]{3,2,1,0:T(8,128)(2,1)} %cotangent.1, s32[2,1,4]{2,1,0:T(1,128)} %lengths.3, ...), custom_call_target="tpu_custom_call" | custom-call | tf_op jit(solution)/shard_map/backward/pallas_call | solution.py:1070
  183.6 4.2 %finish.1 = (bf16[2,512,512]{2,1,0:T(8,128)(2,1)}, bf16[2,512,512]{2,1,0:T(8,128)(2,1)}, f32[32,512]{1,0:T(8,128)}, f32[32,512]{1,0:T(8,128)}, f32[32,512]{1,0:T...) custom-call(bf16[2,512,512]{2,1,0:T(8,128)(2,1)} %get-tuple-element., ...), custom_call_target="tpu_custom_call" | custom-call | tf_op jit(solution)/shard_map/finish/pallas_call | solution.py:1102
